TPU v7x, 32 devices: a whole 2x2x4 slice. The times are simulated.
32 devices in a mesh: dp: 8 (over y, x, core), mp: 4 (over z).
Axes of the slice: x: 2, y: 2, z: 4, core: 2. Of those that a mesh axis runs over, the one named last changes fastest.
Arguments:
- tokens: bfloat16 [8192, 768], P('dp'), may hold values from -6 to 6
- segment_ids: int32 [16, 512], P('dp'), may hold values from 0 to 3, never falling along the last dimension, each value on 1 to 256 neighbouring positions
- buckets: int32 [512, 512], replicated, may hold values from 0 to 319
- qkv_weight: bfloat16 [3, 768, 768], P(None, None, 'mp'), may hold values from -0.21875 to 0.21875
- qv_bias: float32 [2, 768], P(None, 'mp'), may hold values from -3 to 3
- rel_table: float32 [320, 12], P(None, 'mp'), may hold values from -3 to 3
- gate_weight: bfloat16 [64, 8], replicated, may hold values from -0.375 to 0.375
- gate_bias: float32 [8], replicated, may hold values from -2 to 2
- gate_scale: float32 [12], P('mp'), may hold values from 0.5 to 2.5
- out_weight: bfloat16 [768, 768], P('mp'), may hold values from -1.25 to 1.25
- out_bias: float32 [768], replicated, may hold values from -3 to 3
- ln1_gain: float32 [768], replicated, may hold values from 0.1 to 1.9
- ln1_bias: float32 [768], replicated, may hold values from -3 to 3
- fc1_weight: bfloat16 [768, 3072], P(None, 'mp'), may hold values from -0.21875 to 0.21875
- fc1_bias: float32 [3072], P('mp'), may hold values from -3 to 3
- fc2_weight: bfloat16 [3072, 768], P('mp'), may hold values from -0.21875 to 0.21875
- fc2_bias: float32 [768], replicated, may hold values from -3 to 3
- ln2_gain: float32 [768], replicated, may hold values from 0.1 to 1.9
- ln2_bias: float32 [768], replicated, may hold values from -3 to 3
- grad_out: bfloat16 [8192, 768], P('dp'), may hold values from -6 to 6
Outputs:
- output: float32 [8192, 768], P('dp')
- input_grad: float32 [8192, 768], P('dp')
- grad_qkv_weight: float32 [3, 768, 768], P(None, None, 'mp')
- grad_qv_bias: float32 [2, 768], P(None, 'mp')
- grad_rel_table: float32 [320, 12], P(None, 'mp')
- grad_gate_weight: float32 [64, 8], replicated
- grad_gate_bias: float32 [8], replicated
- grad_gate_scale: float32 [12], P('mp')
- grad_out_weight: float32 [768, 768], P('mp')
- grad_out_bias: float32 [768], replicated
- grad_ln1_gain: float32 [768], replicated
- grad_ln1_bias: float32 [768], replicated
- grad_fc1_weight: float32 [768, 3072], P(None, 'mp')
- grad_fc1_bias: float32 [3072], P('mp')
- grad_fc2_weight: float32 [3072, 768], P('mp')
- grad_fc2_bias: float32 [768], replicated
- grad_ln2_gain: float32 [768], replicated
- grad_ln2_bias: float32 [768], replicated
Inputs may be any that keep to these rules, and one draw needn't show every extreme that they name: `segment_ids`: segment numbers never fall along a row of 512 patches, and a segment holds at most 256 patches. `buckets`: one bucket for each pair of positions, the same for every row.
All inputs are finite; a program needn't handle non-finite values.
Results may differ from a plain program's by a relative error of at most 0.02.
Values may be sent and summed in bfloat16 or wider, within the bound.
No kernel may reach another device: no remote copies, remote signals or barrier semaphores. Data moves between devices by JAX's collectives and lax.ppermute only.
A program may use at most 320 MiB of HBM per device.

v0:
```python
import jax
import jax.numpy as jnp
from jax import lax
from jax.sharding import PartitionSpec as P

highest = lax.Precision.HIGHEST
norm_eps = 1e-05
deep_alpha = 24.0**0.25
masked_score = -1e30


def layer_norm(values_in, gain, shift):
    mean_row = jnp.mean(values_in, axis=-1, keepdims=True)
    centred = values_in - mean_row
    spread = jnp.mean(centred * centred, axis=-1, keepdims=True)
    return centred * lax.rsqrt(spread + norm_eps) * gain + shift


def gate_values(heads_in, gate_weight, gate_bias, gate_scale):
    gate_lin = jnp.einsum("thc,cg->thg", heads_in, gate_weight, precision=highest) + gate_bias
    half = gate_lin.shape[-1] // 2
    first_gate = jax.nn.sigmoid(jnp.sum(gate_lin[..., :half], axis=-1))
    second_gate = jax.nn.sigmoid(jnp.sum(gate_lin[..., half:], axis=-1))
    return first_gate * (second_gate * gate_scale - 1.0) + 2.0


def gelu_exact(values_in):
    return jax.nn.gelu(values_in, approximate=False)


def scores_of(queries, keys_all, gate, pos_bias, segment):
    scale = queries.shape[-1] ** (-0.5)
    raw = jnp.einsum("qhd,khd->hqk", queries, keys_all, preferred_element_type=jnp.float32) * scale
    raw = raw + jnp.swapaxes(gate, 0, 1)[:, :, None] * pos_bias
    same = segment[:, None] == segment[None, :]
    return jnp.where(same[None], raw, masked_score)


def body(
    tokens,
    segment_ids,
    buckets,
    qkv_weight,
    qv_bias,
    rel_table,
    gate_weight,
    gate_bias,
    gate_scale,
    out_weight,
    out_bias,
    ln1_gain,
    ln1_bias,
    fc1_weight,
    fc1_bias,
    fc2_weight,
    fc2_bias,
    ln2_gain,
    ln2_bias,
    grad_out,
):
    rows = tokens.shape[0]
    seq_count = segment_ids.shape[0]
    seq_len = segment_ids.shape[1]
    local_heads = rel_table.shape[1]
    head_dim = gate_weight.shape[0]
    width = local_heads * head_dim
    col_start = lax.axis_index("mp") * width
    scale = head_dim ** (-0.5)
    projected = jnp.einsum("td,cde->cte", tokens, qkv_weight, preferred_element_type=jnp.float32)
    queries = (projected[0] + qv_bias[0]).astype(jnp.bfloat16)
    keys_all = projected[1].astype(jnp.bfloat16)
    values_all = (projected[2] + qv_bias[1]).astype(jnp.bfloat16)
    heads_in = (
        lax.dynamic_slice_in_dim(tokens, col_start, width, 1)
        .astype(jnp.float32)
        .reshape(rows, local_heads, head_dim)
    )
    gate, gate_pull = jax.vjp(
        gate_values, heads_in, gate_weight.astype(jnp.float32), gate_bias, gate_scale
    )
    pos_bias = jnp.moveaxis(rel_table[buckets], 2, 0)

    def split_rows(member):
        return member.reshape(seq_count, seq_len, local_heads, head_dim)

    query_rows = split_rows(queries)
    key_rows = split_rows(keys_all)
    value_rows = split_rows(values_all)
    gate_rows = gate.reshape(seq_count, seq_len, local_heads)

    def attend_forward(block):
        part_q, part_k, part_v, segment, part_gate = block
        scores = scores_of(part_q, part_k, part_gate, pos_bias, segment)
        top = jnp.max(scores, axis=-1, keepdims=True)
        weights = jnp.exp(scores - top)
        total = jnp.sum(weights, axis=-1, keepdims=True)
        probs = (weights / total).astype(jnp.bfloat16)
        context = jnp.einsum("hqk,khd->qhd", probs, part_v, preferred_element_type=jnp.float32)
        return (context.astype(jnp.bfloat16), top[..., 0] + jnp.log(total[..., 0]))

    context_rows, log_totals = lax.map(
        attend_forward, (query_rows, key_rows, value_rows, segment_ids, gate_rows)
    )
    context = context_rows.reshape(rows, width)
    attn_part = jnp.dot(context, out_weight, preferred_element_type=jnp.float32)
    attended = lax.psum(attn_part, "mp") + out_bias
    first_sum = deep_alpha * tokens.astype(jnp.float32) + attended
    hidden, ln1_pull = jax.vjp(layer_norm, first_sum, ln1_gain, ln1_bias)
    hidden_low = hidden.astype(jnp.bfloat16)
    pre = jnp.dot(hidden_low, fc1_weight, preferred_element_type=jnp.float32) + fc1_bias
    active, gelu_pull = jax.vjp(gelu_exact, pre)
    active_low = active.astype(jnp.bfloat16)
    ffn_part = jnp.dot(active_low, fc2_weight, preferred_element_type=jnp.float32)
    mixed = deep_alpha * hidden + (lax.psum(ffn_part, "mp") + fc2_bias)
    normed, ln2_pull = jax.vjp(layer_norm, mixed, ln2_gain, ln2_bias)
    grad_mixed, grad_ln2_gain, grad_ln2_bias = ln2_pull(grad_out.astype(jnp.float32))
    grad_fc2_bias = jnp.sum(grad_mixed, axis=0)
    mixed_low = grad_mixed.astype(jnp.bfloat16)
    grad_fc2_weight = jnp.einsum(
        "tf,td->fd", active_low, mixed_low, preferred_element_type=jnp.float32
    )
    grad_active = jnp.einsum("td,fd->tf", mixed_low, fc2_weight, preferred_element_type=jnp.float32)
    (grad_pre,) = gelu_pull(grad_active)
    grad_fc1_bias = jnp.sum(grad_pre, axis=0)
    pre_low = grad_pre.astype(jnp.bfloat16)
    grad_fc1_weight = jnp.einsum(
        "td,tf->df", hidden_low, pre_low, preferred_element_type=jnp.float32
    )
    hidden_part = jnp.einsum("tf,df->td", pre_low, fc1_weight, preferred_element_type=jnp.float32)
    hidden_sum = lax.psum(hidden_part, "mp")
    grad_hidden = deep_alpha * grad_mixed + hidden_sum
    grad_first, grad_ln1_gain, grad_ln1_bias = ln1_pull(grad_hidden)
    grad_out_bias = jnp.sum(grad_first, axis=0)
    first_low = grad_first.astype(jnp.bfloat16)
    grad_out_weight = jnp.einsum(
        "tc,td->cd", context, first_low, preferred_element_type=jnp.float32
    )
    grad_context = jnp.einsum(
        "td,cd->tc", first_low, out_weight, preferred_element_type=jnp.float32
    ).astype(jnp.bfloat16)

    def attend_backward(table_acc, block):
        part_q, part_k, part_v, segment, part_gate, part_log, part_grad = block
        scores = scores_of(part_q, part_k, part_gate, pos_bias, segment)
        probs = jnp.exp(scores - part_log[..., None])
        probs_low = probs.astype(jnp.bfloat16)
        grad_v = jnp.einsum(
            "hqk,qhd->khd", probs_low, part_grad, preferred_element_type=jnp.float32
        )
        grad_probs = jnp.einsum(
            "qhd,khd->hqk", part_grad, part_v, preferred_element_type=jnp.float32
        )
        centre = jnp.sum(probs * grad_probs, axis=-1, keepdims=True)
        grad_scores = (probs * (grad_probs - centre)).astype(jnp.bfloat16)
        grad_q = (
            jnp.einsum("hqk,khd->qhd", grad_scores, part_k, preferred_element_type=jnp.float32)
            * scale
        )
        grad_k = (
            jnp.einsum("hqk,qhd->khd", grad_scores, part_q, preferred_element_type=jnp.float32)
            * scale
        )
        scores_float = grad_scores.astype(jnp.float32)
        grad_gate_rows = jnp.swapaxes(jnp.sum(scores_float * pos_bias, axis=-1), 0, 1)
        table_acc = table_acc + jnp.swapaxes(part_gate, 0, 1)[:, :, None] * scores_float
        return (table_acc, (grad_q, grad_k, grad_v, grad_gate_rows))

    table_start = jnp.zeros((local_heads, seq_len, seq_len), jnp.float32)
    table_acc, (grad_q, grad_k, grad_v, grad_gate) = lax.scan(
        attend_backward,
        table_start,
        (
            query_rows,
            key_rows,
            value_rows,
            segment_ids,
            gate_rows,
            log_totals,
            grad_context.reshape(seq_count, seq_len, local_heads, head_dim),
        ),
    )
    grad_proj = jnp.stack(
        [grad_q.reshape(rows, width), grad_k.reshape(rows, width), grad_v.reshape(rows, width)]
    ).astype(jnp.bfloat16)
    grad_qv_bias = jnp.stack(
        [
            jnp.sum(grad_proj[0].astype(jnp.float32), axis=0),
            jnp.sum(grad_proj[2].astype(jnp.float32), axis=0),
        ]
    )
    grad_qkv_weight = jnp.einsum(
        "td,cte->cde", tokens, grad_proj, preferred_element_type=jnp.float32
    )
    grad_rel_table = jax.ops.segment_sum(
        table_acc.reshape(local_heads, -1).T, buckets.reshape(-1), num_segments=rel_table.shape[0]
    )
    grad_heads, grad_gate_weight, grad_gate_bias, grad_gate_scale = gate_pull(
        grad_gate.reshape(rows, local_heads)
    )
    token_part = jnp.einsum(
        "cte,cde->td", grad_proj, qkv_weight, preferred_element_type=jnp.float32
    )
    head_columns = lax.dynamic_slice_in_dim(token_part, col_start, width, 1) + grad_heads.reshape(
        rows, width
    )
    token_part = lax.dynamic_update_slice_in_dim(token_part, head_columns, col_start, 1)
    token_sum, grad_gate_weight, grad_gate_bias = lax.psum(
        (token_part, grad_gate_weight, grad_gate_bias), "mp"
    )
    input_grad = deep_alpha * grad_first + token_sum
    (
        grad_qkv_weight,
        grad_qv_bias,
        grad_rel_table,
        grad_gate_weight,
        grad_gate_bias,
        grad_gate_scale,
        grad_out_weight,
        grad_out_bias,
        grad_ln1_gain,
        grad_ln1_bias,
        grad_fc1_weight,
        grad_fc1_bias,
        grad_fc2_weight,
        grad_fc2_bias,
        grad_ln2_gain,
        grad_ln2_bias,
    ) = lax.psum(
        (
            grad_qkv_weight,
            grad_qv_bias,
            grad_rel_table,
            grad_gate_weight,
            grad_gate_bias,
            grad_gate_scale,
            grad_out_weight,
            grad_out_bias,
            grad_ln1_gain,
            grad_ln1_bias,
            grad_fc1_weight,
            grad_fc1_bias,
            grad_fc2_weight,
            grad_fc2_bias,
            grad_ln2_gain,
            grad_ln2_bias,
        ),
        "dp",
    )
    return (
        normed,
        input_grad,
        grad_qkv_weight,
        grad_qv_bias,
        grad_rel_table,
        grad_gate_weight,
        grad_gate_bias,
        grad_gate_scale,
        grad_out_weight,
        grad_out_bias,
        grad_ln1_gain,
        grad_ln1_bias,
        grad_fc1_weight,
        grad_fc1_bias,
        grad_fc2_weight,
        grad_fc2_bias,
        grad_ln2_gain,
        grad_ln2_bias,
    )


def solution(mesh):
    in_specs = (
        P("dp", None),
        P("dp", None),
        P(),
        P(None, None, "mp"),
        P(None, "mp"),
        P(None, "mp"),
        P(),
        P(),
        P("mp"),
        P("mp", None),
        P(),
        P(),
        P(),
        P(None, "mp"),
        P("mp"),
        P("mp", None),
        P(),
        P(),
        P(),
        P("dp", None),
    )
    out_specs = (
        P("dp", None),
        P("dp", None),
        P(None, None, "mp"),
        P(None, "mp"),
        P(None, "mp"),
        P(),
        P(),
        P("mp"),
        P("mp", None),
        P(),
        P(),
        P(),
        P(None, "mp"),
        P("mp"),
        P("mp", None),
        P(),
        P(),
        P(),
    )
    return jax.shard_map(body, mesh=mesh, in_specs=in_specs, out_specs=out_specs, check_vma=False)
```

profile of v0, /device:TPU:0, one launch (start us, length us, event | category | flops | bytes accessed | tf_op | source)
XLA Modules:
  0.0 2959.5 jit_solution(11185507131816073557)
XLA Ops:
  7.3 2.9 convolution_bitcast_fusion.1
  16.8 2.7 squeeze.44
  20.5 2.7 squeeze.43
  23.2 865.9 %gather_fusion = f32[262144,3]{1,0:T(8,128)} fusion(f32[320,3]{1,0:T(8,128)S(1)} %copy.66, s32[262144]{0:T(1024)S(1)} %broadcast_clamp_fusion), kind=kCustom, calls=%fused_computation | custom fusion | bytes 7340032 | tf_op jit(solution)/shard_map/gather | solution.py:81
  889.1 71.4 %copy.67 = f32[512,512,3]{0,1,2:T(8,128)} copy(f32[512,512,3]{2,1,0:T(8,128)} %bitcast.15) | data formatting | bytes 6291456 | tf_op jit(solution)/shard_map/gather | solution.py:81
  961.3 1.4 fusion.65
  962.8 11.1 while.31
  963.1 2.9 fusion.137
  968.6 2.9 fusion.137
  975.4 2.3 fusion.96
  977.9 123.6 %all-reduce.11.cloned.1.call-done = f32[1024,768]{1,0:T(8,128)} async-done(((f32[1024,768]{1,0:T(8,128)}), f32[1024,768]{1,0:T(8,128)}) %all-reduce.11.cloned.1.call-update) | async-done | bytes 3145744 | tf_op jit(solution)/shard_map/psum | solution.py:106
  1101.5 2.9 fusion.90
  1105.3 9.7 multiply_convert_fusion.1
  1116.1 3.1 fusion.97
  1119.3 120.2 %all-reduce.13.cloned.1.call-done = f32[1024,768]{1,0:T(8,128)} async-done(((f32[1024,768]{1,0:T(8,128)}), f32[1024,768]{1,0:T(8,128)}) %all-reduce.13.cloned.1.call-update) | async-done | bytes 3145744 | tf_op jit(solution)/shard_map/psum | solution.py:114
  1239.5 3.9 fusion.88
  1244.8 1.8 fusion.51
  1246.7 2.8 fusion.87
  1249.9 2.3 copy-done.87
  1252.1 3.2 fusion.93
  1256.5 3.1 fusion.69
  1260.1 119.7 %all-reduce.15.cloned.1.call-done = f32[1024,768]{1,0:T(8,128)} async-done(((f32[1024,768]{1,0:T(8,128)}), f32[1024,768]{1,0:T(8,128)}) %all-reduce.15.cloned.1.call-update) | async-done | bytes 3145744 | tf_op jit(solution)/shard_map/psum | solution.py:130
  1379.8 5.5 multiply_reduce_fusion.1
  1385.3 1.5 fusion.86
  1386.8 1.7 copy-done.7
  1389.6 21.4 while.32
  1392.2 1.4 multiply_reduce_fusion.7
  1397.1 1.5 fusion.150
  1398.6 1.7 copy-done.3
  1407.7 1.5 fusion.150
  1409.2 1.7 copy-done.3
  1413.8 1.5 copy.73
  1418.7 1.5 copy.76
  1421.4 2.6 convolution_bitcast_fusion
  1424.0 1.7 copy-done.12
  1426.0 5.8 dynamic_update_slice.25
  1433.3 5.0 fusion.83
  1438.3 3.3 fusion.67
  1441.7 1.4 fusion.85
  1443.6 2.3 fusion.61
  1447.4 3.7 copy.78
  1451.1 6.0 copy.91
  1457.2 58.4 %copy.79 = f32[262144,3]{1,0:T(8,128)} copy(f32[262144,3]{0,1:T(4,128)} %bitcast.203) | data formatting | bytes 6291456 | tf_op jit(solution)/shard_map/transpose | solution.py:195
  1515.6 1387.8 %scatter_custom_fusion = f32[320,3]{1,0:T(8,128)} fusion(s32[262144]{0:T(1024)S(1)} %bitcast.213, f32[262144,3]{1,0:T(8,128)} %copy.79, f32[]{:T(128)} %constant.71.clone.1), kind=kCustom, calls=%fused_computation.132 | custom fusion | flops 786432 | bytes 4352 | tf_op jit(solution)/shard_map/scatter-add | solution.py:194
  2903.9 9.5 all-reduce.4
  2914.7 5.1 add_reduce_fusion
  2919.8 25.6 all-reduce.2
  2946.2 2.9 copy.142
  (301 shorter events, 52.0 us)
Async XLA Ops:
  7.2 1097.8 %copy-start = (bf16[768,768]{1,0:T(8,128)(2,1)S(1)}, bf16[768,768]{1,0:T(8,128)(2,1)}, u32[]{:S(2)}) copy-start(bf16[768,768]{1,0:T(8,128)(2,1)} %param.37) | copy-start | bytes 3538948
  7.2 1094.3 %all-reduce.11.cloned.1.call-start = ((), (), s32[]{:S(2)}) async-start(), calls=%async_computation | async-start | bytes 6291456 | tf_op jit(solution)/shard_map/psum | solution.py:106
  10.2 5.1 copy-start.65
  10.2 5.1 copy-start.78
  11.0 5.2 copy-start.13
  889.1 71.5 %copy-start.42 = (f32[1024,3]{0,1:T(4,128)S(1)}, f32[1024,3]{0,1:T(4,128)}, u32[]{:S(2)}) copy-start(f32[1024,3]{0,1:T(4,128)} %get-tuple-element.282) | copy-start | bytes 36868
  889.1 71.5 %copy-start.43 = (f32[1024,3]{0,1:T(4,128)S(1)}, f32[1024,3]{0,1:T(4,128)}, u32[]{:S(2)}) copy-start(f32[1024,3]{0,1:T(4,128)} %get-tuple-element.283) | copy-start | bytes 36868
  889.1 72.1 %copy-start.76 = (f32[3]{0:T(128)S(1)}, f32[3]{0:T(128)}, u32[]{:S(2)}) copy-start(f32[3]{0:T(128)} %param.32) | copy-start | bytes 40
  889.1 72.2 %copy-start.23 = (f32[2,512,3,64]{1,0,3,2:T(2,128)S(1)}, f32[2,512,3,64]{1,0,3,2:T(2,128)}, u32[]{:S(2)}) copy-start(f32[2,512,3,64]{1,0,3,2:T(2,128)} %squeeze.44) | copy-start | bytes 2359300
  889.1 72.2 %copy-start.67 = (f32[3,64]{1,0:T(4,128)S(1)}, f32[3,64]{1,0:T(4,128)}, u32[]{:S(2)}) copy-start(f32[3,64]{1,0:T(4,128)} %add.218) | copy-start | bytes 2308
  889.1 72.2 %copy-start.68 = (f32[3,64]{1,0:T(4,128)S(1)}, f32[3,64]{1,0:T(4,128)}, u32[]{:S(2)}) copy-start(f32[3,64]{1,0:T(4,128)} %add.215) | copy-start | bytes 2308
  889.1 73.6 %copy-start.9 = (bf16[2,512,3,64]{1,3,2,0:T(8,128)(2,1)S(1)}, bf16[2,512,3,64]{1,3,2,0:T(8,128)(2,1)}, u32[]{:S(2)}) copy-start(bf16[2,512,3,64]{1,3,2,0:T(8,128)(2,1)} %copy.68) | copy-start | bytes 1179652
  889.1 73.6 %copy-start.48 = (s32[2,512]{1,0:T(2,128)S(1)}, s32[2,512]{1,0:T(2,128)}, u32[]{:S(2)}) copy-start(s32[2,512]{1,0:T(2,128)} %param.25) | copy-start | bytes 12292
  962.8 12.6 copy-start.28
  975.3 126.2 %copy-start.70 = (f32[768]{0:T(1024)S(1)}, f32[768]{0:T(1024)}, u32[]{:S(2)}) copy-start(f32[768]{0:T(1024)} %param.34) | copy-start | bytes 9220
  977.7 261.8 %all-reduce.13.cloned.1.call-start = ((), (), s32[]{:S(2)}) async-start(), calls=%async_computation.1 | async-start | bytes 6291456 | tf_op jit(solution)/shard_map/psum | solution.py:114
  1104.5 10.5 copy-start.4
  1104.5 280.8 %copy-start.46 = (f32[1024]{0:T(1024)}, f32[1024]{0:T(1024)S(1)}, u32[]{:S(2)}) copy-start(f32[1024]{0:T(1024)S(1)} %broadcast_multiply_fusion.1) | copy-start | bytes 12292
  1105.3 280.0 %copy-start.49 = (f32[1024]{0:T(1024)}, f32[1024]{0:T(1024)S(1)}, u32[]{:S(2)}) copy-start(f32[1024]{0:T(1024)S(1)} %fusion.77) | copy-start | bytes 12292
  1105.3 10.8 copy-start.79
  1119.2 120.3 %copy-start.71 = (f32[768]{0:T(1024)S(1)}, f32[768]{0:T(1024)}, u32[]{:S(2)}) copy-start(f32[768]{0:T(1024)} %param.40) | copy-start | bytes 9220
  1119.2 260.6 %all-reduce.15.cloned.1.call-start = ((), (), s32[]{:S(2)}) async-start(), calls=%async_computation.2 | async-start | bytes 6291456 | tf_op jit(solution)/shard_map/psum | solution.py:130
  1246.7 5.5 copy-start.87
  1249.5 5.8 copy-start.10
  1249.5 130.3 %copy-start.63 = (f32[1024]{0:T(1024)}, f32[1024]{0:T(1024)S(1)}, u32[]{:S(2)}) copy-start(f32[1024]{0:T(1024)S(1)} %negate_multiply_fusion.2) | copy-start | bytes 12292
  1259.6 1655.1 %all-reduce.17.cloned.1.call-start = ((), (), s32[]{:S(2)}) async-start(), calls=%async_computation.3 | async-start | bytes 6291456 | tf_op jit(solution)/shard_map/psum | solution.py:207
  1379.8 5.5 copy-start.5
  1411.1 6.3 copy-start.66
  1413.8 6.5 copy-start.19
  1426.0 6.0 copy-start.64
  1431.9 6.4 copy-start.47
  1431.9 6.4 copy-start.50
  1431.9 6.4 copy-start.56
  1431.9 6.4 copy-start.74
  1431.9 1514.3 %all-reduce.19.cloned.1.call-start = ((), (), s32[]{:S(2)}) async-start(), calls=%async_computation.4 | async-start | bytes 14155776 | tf_op jit(solution)/shard_map/psum | solution.py:228
  1433.3 5.1 copy-start.85
  1457.1 1446.4 %copy-start.18 = (bf16[1024,192]{0,1:T(8,128)(2,1)S(1)}, bf16[1024,192]{0,1:T(8,128)(2,1)}, u32[]{:S(2)}) copy-start(bf16[1024,192]{0,1:T(8,128)(2,1)} %copy-done.17) | copy-start | bytes 1179652
  1457.1 1456.3 %copy-start.20 = (bf16[1,1024,192]{1,2,0:T(8,128)(2,1)S(1)}, bf16[1,1024,192]{1,2,0:T(8,128)(2,1)}, u32[]{:S(2)}) copy-start(bf16[1,1024,192]{1,2,0:T(8,128)(2,1)} %copy-done.19) | copy-start | bytes 1179652
  1457.1 1456.5 %copy-start.22 = (bf16[1,1024,192]{1,2,0:T(8,128)(2,1)S(1)}, bf16[1,1024,192]{1,2,0:T(8,128)(2,1)}, u32[]{:S(2)}) copy-start(bf16[1,1024,192]{1,2,0:T(8,128)(2,1)} %copy-done.21) | copy-start | bytes 1179652
  1457.1 1456.6 %copy-start.39 = (f32[1024,3]{0,1:T(4,128)S(1)}, f32[1024,3]{0,1:T(4,128)}, u32[]{:S(2)}) copy-start(f32[1024,3]{0,1:T(4,128)} %copy-done.38) | copy-start | bytes 36868
  1457.1 1456.6 %copy-start.41 = (f32[1024,3]{0,1:T(4,128)S(1)}, f32[1024,3]{0,1:T(4,128)}, u32[]{:S(2)}) copy-start(f32[1024,3]{0,1:T(4,128)} %copy-done.40) | copy-start | bytes 36868
  2914.6 5.2 copy-start.29
  2914.6 5.2 copy-start.58
  2914.6 5.2 copy-start.59
  2914.6 5.2 copy-start.60
  2914.7 5.2 copy-start.61
  2914.7 5.2 copy-start.62
  2914.7 5.1 copy-start.75
  (56 other events, 109.3 us)
Sparse Core Ops, SparseCore 0:
  977.8 123.6 all-reduce.10
  1119.3 120.0 all-reduce.12
  1259.7 120.0 all-reduce.14
  1432.0 119.9 all-reduce.16
  1556.7 112.4 all-reduce.18
where the time goes:
time: 2970 us; the launch traced here: 2960 us
  other arithmetic  1430 us (48%)
  local copies, waits for them, and re-layouts  1060 us (36%)
  waiting for transfers between devices  364 us (12%)
  matrix products  55.9 us (2%)
  blocking collectives  35.2 us (1%)
    scatter-add x1, other arithmetic, body(): jax.ops.segment_sum(table_acc.reshape(local_heads, -1).T, buckets.reshape...  1390 us
    gather x2, local copies, waits for them, and re-layouts, body(): pos_bias = jnp.moveaxis(rel_table[buckets], 2, 0)  937 us
    psum x1, waiting for transfers between devices, body(): attended = lax.psum(attn_part, 'mp') + out_bias  124 us
    psum x1, waiting for transfers between devices, body(): mixed = deep_alpha * hidden + (lax.psum(ffn_part, 'mp') + fc2_bias)  120 us
    psum x1, waiting for transfers between devices, body(): hidden_sum = lax.psum(hidden_part, 'mp')  120 us
  transfers between devices with their start and end apart: 5, of which 3 were waited for; matrix products, arithmetic and copies ran while one was open for 50% of the time, Pallas kernels for 0%

commit v1 on v0

v1 whole, which is shorter than its diff:
```python
import functools

import jax
import jax.numpy as jnp
from jax import lax
from jax.experimental import pallas as pl
from jax.experimental.pallas import tpu as pltpu
from jax.sharding import PartitionSpec as P

norm_eps = 1e-05
deep_alpha = 24.0**0.25
masked_score = -1e30
bf = jnp.bfloat16
f32 = jnp.float32
LANES = 128


def nn(a, b):
    return lax.dot_general(a, b, (((1,), (0,)), ((), ())), preferred_element_type=f32)


def nt(a, b):
    return lax.dot_general(a, b, (((1,), (1,)), ((), ())), preferred_element_type=f32)


def params(mib):
    return pltpu.CompilerParams(vmem_limit_bytes=mib * 1024 * 1024)


def bias_kernel(heads, chunks, buckets_ref, table_ref, out_ref):
    rows, cols = buckets_ref.shape

    def group(g, carry):
        at = pl.ds(pl.multiple_of(g * 8, 8), 8)
        for c in range(cols // LANES):
            lanes = pl.ds(c * LANES, LANES)
            idx = buckets_ref[at, lanes]
            low = idx & (LANES - 1)
            high = idx >> 7
            for h in range(heads):
                got = None
                for k in range(chunks):
                    line = jnp.broadcast_to(table_ref[h, pl.ds(k, 1), :], (8, LANES))
                    part = jnp.take_along_axis(line, low, axis=1, mode="promise_in_bounds")
                    got = part if got is None else jnp.where(high == k, part, got)
                out_ref[h, at, lanes] = got
        return carry

    lax.fori_loop(0, rows // 8, group, 0)


def bias_of(buckets_t, table):
    heads, chunks, _ = table.shape
    seq = buckets_t.shape[0]
    rows = 64
    return pl.pallas_call(
        functools.partial(bias_kernel, heads, chunks),
        grid=(seq // rows,),
        in_specs=[
            pl.BlockSpec((rows, seq), lambda i: (i, 0)),
            pl.BlockSpec((heads, chunks, LANES), lambda i: (0, 0, 0)),
        ],
        out_specs=pl.BlockSpec((heads, rows, seq), lambda i: (0, i, 0)),
        out_shape=jax.ShapeDtypeStruct((heads, seq, seq), f32),
        name="pos_bias",
    )(buckets_t, table)


def attend_kernel(
    heads, hd, gates, idx_ref, x_ref, w_ref, gb_ref, qvb_ref, pos_ref, segq_ref, segk_ref, gbias_ref, gscale_ref,
    qkv_ref, ctx_ref, out_t_ref, lse_ref, gate_ref, mask, sc, pr,
):
    r = pl.program_id(0)
    width = heads * hd
    seq = x_ref.shape[0]
    x = x_ref[...]
    wide = nt(w_ref[0], x) + qvb_ref[0]
    qkv_ref[0, 0, pl.ds(0, width), :] = wide[:width].astype(bf) * bf(hd**-0.5)
    qkv_ref[0, 0, pl.ds(width, 2 * width), :] = wide[width:].astype(bf)
    lin = nt(gb_ref[0], x)
    half = gates // 2
    for c in range(seq // LANES):
        lanes = pl.ds(c * LANES, LANES)
        mask[:, lanes] = jnp.where(segk_ref[0] == segq_ref[0, :, lanes], 0.0, masked_score)
    for h in range(heads):
        at = pl.ds(h * hd, hd)
        q_t = qkv_ref[0, 0, at, :]
        k_t = qkv_ref[0, 0, pl.ds(width + h * hd, hd), :]
        v_t = qkv_ref[0, 0, pl.ds(2 * width + h * hd, hd), :]
        first = jax.nn.sigmoid(jnp.sum(lin[h * gates : h * gates + half], axis=0, keepdims=True) + gbias_ref[0])
        second = jax.nn.sigmoid(
            jnp.sum(lin[h * gates + half : (h + 1) * gates], axis=0, keepdims=True) + gbias_ref[1]
        )
        gate = first * (second * gscale_ref[idx_ref[r], h] - 1.0) + 2.0
        gate_ref[0, 0, pl.ds(h, 1), :] = first
        gate_ref[0, 0, pl.ds(heads + h, 1), :] = second
        sc[h % 2] = nn(k_t.T, q_t)
        for c in range(seq // LANES):
            lanes = pl.ds(c * LANES, LANES)
            s = sc[h % 2, :, lanes] + pos_ref[0, h, :, lanes] * gate[:, c * LANES : (c + 1) * LANES] + mask[:, lanes]
            top = jnp.max(s, axis=0, keepdims=True)
            p = jnp.exp(s - top)
            total = jnp.sum(p, axis=0, keepdims=True)
            pr[h % 2, :, lanes] = p.astype(bf)
            lse_ref[0, 0, pl.ds(h, 1), lanes] = top + jnp.log(total)
            lse_ref[0, 0, pl.ds(heads + h, 1), lanes] = 1.0 / total
        out_t_ref[0, 0, at, :] = nn(v_t, pr[h % 2]) * lse_ref[0, 0, pl.ds(heads + h, 1), :]
    ctx_ref[0] = out_t_ref[0, 0].T.astype(bf)


def attend_back_kernel(
    heads, hd, idx_ref, x_ref, w_ref, gsum_ref, pos_ref, segq_ref, segk_ref, gscale_ref, qkv_ref, out_t_ref, lse_ref,
    gate_ref, dctx_ref, first_ref,
    grad_ref, dw_ref, dqv_ref, dgw_ref, dgate_ref, table_ref, mask, sc, dp, pr, ds, wide,
):
    r = pl.program_id(0)
    row = pl.program_id(1)
    width = heads * hd
    seq = x_ref.shape[0]
    for c in range(seq // LANES):
        lanes = pl.ds(c * LANES, LANES)
        mask[:, lanes] = jnp.where(segk_ref[0] == segq_ref[0, :, lanes], 0.0, masked_score)
    wide[...] = jnp.zeros_like(wide)
    dgate_ref[0, 0] = jnp.zeros_like(dgate_ref[0, 0])
    for h in range(heads):
        at = pl.ds(h * hd, hd)
        q_t = qkv_ref[0, 0, at, :]
        k_t = qkv_ref[0, 0, pl.ds(width + h * hd, hd), :]
        v_t = qkv_ref[0, 0, pl.ds(2 * width + h * hd, hd), :]
        g_t = dctx_ref[0, at, :]
        b = h % 2
        sc[b] = nn(k_t.T, q_t)
        dp[b] = nn(v_t.T, g_t)
        first = gate_ref[0, 0, pl.ds(h, 1), :]
        second = gate_ref[0, 0, pl.ds(heads + h, 1), :]
        scale = gscale_ref[idx_ref[r], h]
        gate = first * (second * scale - 1.0) + 2.0
        centre = jnp.sum(g_t.astype(f32) * out_t_ref[0, 0, at, :], axis=0, keepdims=True)
        lse = lse_ref[0, 0, pl.ds(h, 1), :]
        parts = []
        for c in range(seq // LANES):
            lanes = pl.ds(c * LANES, LANES)
            cut = slice(c * LANES, (c + 1) * LANES)
            pos = pos_ref[0, h, :, lanes]
            p = jnp.exp(sc[b, :, lanes] + (pos * gate[:, cut] - lse[:, cut]) + mask[:, lanes])
            pr[b, :, lanes] = p.astype(bf)
            d = p * (dp[b, :, lanes] - centre[:, cut])
            ds[b, :, lanes] = d.astype(bf)
            parts.append(jnp.sum(d * pos, axis=0, keepdims=True))
        dgate = jnp.concatenate(parts, axis=1)

        @pl.when(r == 0)
        def _():
            @pl.when(row == 0)
            def _():
                table_ref[h] = gate * ds[b].astype(f32)

            @pl.when(row != 0)
            def _():
                table_ref[h] += gate * ds[b].astype(f32)

        wide[at, :] = (nn(k_t, ds[b]) * hd**-0.5).astype(bf)
        wide[pl.ds(width + h * hd, hd), :] = nt(q_t, ds[b]).astype(bf)
        wide[pl.ds(2 * width + h * hd, hd), :] = nt(g_t, pr[b]).astype(bf)
        dfirst = dgate * (second * scale - 1.0) * first * (1.0 - first)
        dsecond = dgate * first * scale * second * (1.0 - second)
        dgate_ref[0, 0, pl.ds(h, 1), :] = dfirst
        dgate_ref[0, 0, pl.ds(heads + h, 1), :] = dsecond
        dgate_ref[0, 0, pl.ds(8 + h, 1), :] = dgate * first * second
    x = x_ref[...]
    low_gate = dgate_ref[0, 0].astype(bf)
    wide[pl.ds(3 * width, 16), :] = low_gate

    @pl.when(row == 0)
    def _():
        dgw_ref[0] = nn(low_gate, x)

    @pl.when(row != 0)
    def _():
        dgw_ref[0] += nn(low_gate, x)

    lines = pl.ds(pl.multiple_of(row * seq, seq), seq)
    part = nn(wide[pl.ds(0, 3 * width), :].T, w_ref[0]) + nn(wide[pl.ds(3 * width, 16), :].T, gsum_ref[0])

    @pl.when(r == 0)
    def _():
        grad_ref[lines, :] = deep_alpha * first_ref[lines, :] + part
        dqv_ref[0] = wide[pl.ds(0, 3 * width), :]

        @pl.when(row == 0)
        def _():
            dw_ref[...] = nn(wide[pl.ds(0, 3 * width), :], x)

        @pl.when(row != 0)
        def _():
            dw_ref[...] += nn(wide[pl.ds(0, 3 * width), :], x)

    @pl.when(r != 0)
    def _():
        grad_ref[lines, :] += part


def norm_stats(v):
    mean = jnp.mean(v, axis=-1, keepdims=True)
    cen = v - mean
    rs = lax.rsqrt(jnp.mean(cen * cen, axis=-1, keepdims=True) + norm_eps)
    return cen * rs, rs


def norm_back(g, n, rs, gain):
    gn = g * gain
    return rs * (gn - jnp.mean(gn, axis=-1, keepdims=True) - n * jnp.mean(gn * n, axis=-1, keepdims=True))


def gelu_pair(x):
    e = jnp.exp(x * x * -0.5)
    t = 1.0 / (1.0 + (0.3275911 * 0.5**0.5) * jnp.abs(x))
    poly = t * (0.5 * 0.254829592 + t * (0.5 * -0.284496736 + t * (0.5 * 1.421413741 + t * (0.5 * -1.453152027 + t * (0.5 * 1.061405429)))))
    tail = poly * e
    cdf = jnp.where(x > 0.0, 1.0 - tail, tail)
    return x * cdf, cdf + x * e * 0.3989422804014327


def layer_kernel(
    idx_ref, ctx_ref, x_ref, go_ref, ow_ref, w1_ref, b1_ref, w2_ref, vec_ref,
    out_ref, first_ref, dctx_ref, hid_low_ref, mix_low_ref, first_low_ref, act_ref, pre_low_ref, sums_ref,
    act, slope, plow,
):
    step = pl.program_id(0)
    parts, units, feats = w1_ref.shape
    rows = x_ref.shape[0]
    own = idx_ref[0]
    vec = vec_ref[...]
    out_bias, gain1, bias1, bias2, gain2, beta2 = (vec[i : i + 1] for i in range(6))
    total = deep_alpha * x_ref[...].astype(f32) + out_bias
    for c in range(parts):
        total = total + nn(ctx_ref[c], ow_ref[c])
    n1, rs1 = norm_stats(total)
    hidden = n1 * gain1 + bias1
    hid_low = hidden.astype(bf)
    hid_low_ref[...] = hid_low
    block = 256
    for c in range(parts):
        for u in range(0, units, block):
            pre = nt(hid_low, w1_ref[c, pl.ds(u, block), :]) + b1_ref[c, :, pl.ds(u, block)]
            a, s = gelu_pair(pre)
            act[c, :, pl.ds(u, block)] = a.astype(bf)
            slope[c, :, pl.ds(u, block)] = s.astype(bf)
    mixed = deep_alpha * hidden + bias2
    for c in range(parts):
        mixed = mixed + nn(act[c], w2_ref[c])
    act_ref[...] = act[own]
    n2, rs2 = norm_stats(mixed)
    out_ref[...] = n2 * gain2 + beta2
    g = go_ref[...].astype(f32)
    grad_mixed = norm_back(g, n2, rs2, gain2)
    mix_low = grad_mixed.astype(bf)
    mix_low_ref[...] = mix_low
    bias_sums = []
    for c in range(parts):
        line = []
        for u in range(0, units, block):
            d = nt(mix_low, w2_ref[c, pl.ds(u, block), :]) * slope[c, :, pl.ds(u, block)].astype(f32)
            line.append(jnp.sum(d, axis=0, keepdims=True))
            plow[c, :, pl.ds(u, block)] = d.astype(bf)
        bias_sums.append(jnp.concatenate(line, axis=1))
    grad_hidden = deep_alpha * grad_mixed
    for c in range(parts):
        grad_hidden = grad_hidden + nn(plow[c], w1_ref[c])
    pre_low_ref[...] = plow[own]
    b1_sum = bias_sums[0]
    for c in range(1, parts):
        b1_sum = jnp.where(own == c, bias_sums[c], b1_sum)
    grad_first = norm_back(grad_hidden, n1, rs1, gain1)
    first_ref[...] = grad_first
    first_low = grad_first.astype(bf)
    first_low_ref[...] = first_low
    for c in range(parts):
        dctx_ref[c] = nt(ow_ref[c], first_low).astype(bf)

    def col(v):
        return jnp.sum(v, axis=0, keepdims=True)

    sums = jnp.concatenate(
        [
            col(g * n2), col(g), col(grad_mixed), col(grad_hidden * n1), col(grad_hidden), col(grad_first), b1_sum,
            jnp.zeros_like(b1_sum),
        ],
        axis=0,
    )

    @pl.when(step == 0)
    def _():
        sums_ref[...] = sums

    @pl.when(step != 0)
    def _():
        sums_ref[...] += sums


def table_kernel(heads, tops, lows, buckets_ref, val_ref, out_ref):
    rows, cols = buckets_ref.shape

    @pl.when(pl.program_id(0) == 0)
    def _():
        out_ref[...] = jnp.zeros_like(out_ref)

    top_id = lax.broadcasted_iota(jnp.int32, (tops, cols), 0)
    low_id = lax.broadcasted_iota(jnp.int32, (lows, cols), 0)

    def group(g, acc):
        at = pl.ds(pl.multiple_of(g * 8, 8), 8)
        idx = buckets_ref[at, :]
        high = idx >> 4
        low = idx & 15
        vals = [val_ref[h, at, :] for h in range(heads)]
        for i in range(8):
            a = (high[i : i + 1] == top_id).astype(f32).astype(bf)
            hit = low[i : i + 1] == low_id
            b = jnp.concatenate([jnp.where(hit, v[i : i + 1], 0.0) for v in vals], axis=0).astype(bf)
            acc = acc + nt(a, b)
        return acc

    out_ref[...] += lax.fori_loop(0, rows // 8, group, jnp.zeros(out_ref.shape, f32))


def table_grad(buckets_t, values, size):
    heads, seq, _ = values.shape
    lows = 16
    tops = -(-size // lows // 8) * 8
    rows = 64
    out = pl.pallas_call(
        functools.partial(table_kernel, heads, tops, lows),
        grid=(seq // rows,),
        in_specs=[
            pl.BlockSpec((rows, seq), lambda i: (i, 0)),
            pl.BlockSpec((heads, rows, seq), lambda i: (0, i, 0)),
        ],
        out_specs=pl.BlockSpec((tops, heads * lows), lambda i: (0, 0)),
        out_shape=jax.ShapeDtypeStruct((tops, heads * lows), f32),
        name="table_grad",
    )(buckets_t, values)
    return out.reshape(tops, heads, lows).transpose(0, 2, 1).reshape(tops * lows, heads)[:size]


def body(
    n_dp, n_mp,
    tokens, segment_ids, buckets, qkv_weight, qv_bias, rel_table, gate_weight, gate_bias, gate_scale, out_weight,
    out_bias, ln1_gain, ln1_bias, fc1_weight, fc1_bias, fc2_weight, fc2_bias, ln2_gain, ln2_bias, grad_out,
):
    rows, feats = tokens.shape
    seqs, seq = segment_ids.shape
    size, heads = rel_table.shape
    hd, gates = gate_weight.shape
    width = heads * hd
    units = fc1_weight.shape[1]
    me = lax.axis_index("mp")
    dp = lax.axis_index("dp")
    order = (me + jnp.arange(n_mp)) % n_mp
    idx = order.astype(jnp.int32)

    small = jnp.concatenate([rel_table.T.reshape(-1), fc1_bias, qv_bias.reshape(-1), gate_scale])
    small = lax.all_gather(small, "mp")
    cuts = [size * heads, units, 2 * width, heads]
    ends = [sum(cuts[:i]) for i in range(len(cuts) + 1)]
    tables, b1, qvb, scales = (small[:, ends[i] : ends[i + 1]] for i in range(4))
    chunks = -(-size // LANES)
    tables = jnp.pad(tables.reshape(n_mp * heads, size), ((0, 0), (0, chunks * LANES - size)))
    tables = tables.reshape(n_mp * heads, chunks, LANES)
    b1 = b1.reshape(n_mp, 1, units)
    qvb = qvb.reshape(n_mp, 2, width)
    qvb = jnp.concatenate([qvb[:, 0], jnp.zeros_like(qvb[:, 0]), qvb[:, 1]], axis=1)[:, :, None]

    def gathered(w):
        per = w.shape[0] // n_dp
        mine = lax.dynamic_slice_in_dim(w, dp * per, per, 0)
        return lax.all_gather(mine, ("mp", "dp"), tiled=True).reshape(n_mp, w.shape[0], w.shape[1])

    wqkv = gathered(qkv_weight.transpose(0, 2, 1).reshape(3 * width, feats))
    ow = gathered(out_weight)
    w1 = gathered(fc1_weight.T)
    w2 = gathered(fc2_weight)

    eye = jnp.eye(n_mp * heads, dtype=bf).reshape(n_mp, heads, 1, n_mp * heads, 1)
    gb = (eye * gate_weight.T.reshape(1, 1, gates, 1, hd)).reshape(n_mp, heads * gates, feats)
    gb = jnp.pad(gb, ((0, 0), (0, 32 - heads * gates), (0, 0)))
    gw = gate_weight.astype(f32).T
    halves = jnp.stack([gw[: gates // 2].sum(0), gw[gates // 2 :].sum(0)]).astype(bf)
    gsum = (eye.reshape(n_mp, 1, heads, n_mp * heads, 1) * halves.reshape(1, 2, 1, 1, hd)).reshape(n_mp, 2 * heads, feats)
    gsum = jnp.pad(gsum, ((0, 0), (0, 16 - 2 * heads), (0, 0)))
    gbias = jnp.stack([gate_bias[: gates // 2].sum(), gate_bias[gates // 2 :].sum()])

    buckets_t = buckets.T
    pos = bias_of(buckets_t, tables).reshape(n_mp, heads, seq, seq)
    segq = segment_ids[:, None, :]
    segk = segment_ids[:, :, None]

    whole = lambda *shape: pl.BlockSpec(shape, lambda *_: (0,) * len(shape))
    smem = pl.BlockSpec(memory_space=pltpu.SMEM)
    by_r = lambda *shape: pl.BlockSpec((1,) + shape, lambda r, s, ix: (ix[r],) + (0,) * len(shape))
    by_rs = lambda *shape: pl.BlockSpec((1, 1) + shape, lambda r, s, ix: (ix[r], s) + (0,) * len(shape))
    x_spec = pl.BlockSpec((seq, feats), lambda r, s, ix: (s, 0))
    segq_spec = pl.BlockSpec((1, 1, seq), lambda r, s, ix: (s, 0, 0))
    segk_spec = pl.BlockSpec((1, seq, 1), lambda r, s, ix: (s, 0, 0))
    sds = jax.ShapeDtypeStruct

    qkv_t, ctx, out_t, lse, gate = pl.pallas_call(
        functools.partial(attend_kernel, heads, hd, gates),
        grid_spec=pltpu.PrefetchScalarGridSpec(
            num_scalar_prefetch=1,
            grid=(n_mp, seqs),
            in_specs=[
                x_spec, by_r(3 * width, feats), by_r(32, feats), by_r(3 * width, 1), by_r(heads, seq, seq), segq_spec,
                segk_spec, smem, smem,
            ],
            out_specs=[
                by_rs(3 * width, seq),
                pl.BlockSpec((1, seq, width), lambda r, s, ix: (ix[r], s, 0)),
                by_rs(width, seq), by_rs(8, seq), by_rs(8, seq),
            ],
            scratch_shapes=[
                pltpu.VMEM((seq, seq), f32), pltpu.VMEM((2, seq, seq), f32), pltpu.VMEM((2, seq, seq), bf),
            ],
        ),
        out_shape=[
            sds((n_mp, seqs, 3 * width, seq), bf), sds((n_mp, rows, width), bf), sds((n_mp, seqs, width, seq), f32),
            sds((n_mp, seqs, 8, seq), f32), sds((n_mp, seqs, 8, seq), f32),
        ],
        compiler_params=params(56),
        name="attend",
    )(idx, tokens, wqkv, gb, qvb, pos, segq, segk, gbias, scales)

    vec = jnp.stack([out_bias, ln1_gain, ln1_bias, fc2_bias, ln2_gain, ln2_bias, out_bias, out_bias])
    tile = 256
    row = lambda n: pl.BlockSpec((tile, n), lambda i, ix: (i, 0))
    once = lambda *shape: pl.BlockSpec(shape, lambda *_: (0,) * len(shape), pipeline_mode=pl.Buffered(1))
    (normed, grad_first, dctx, hid_low, mix_low, first_low, act_own, pre_own, sums) = pl.pallas_call(
        layer_kernel,
        grid_spec=pltpu.PrefetchScalarGridSpec(
            num_scalar_prefetch=1,
            grid=(rows // tile,),
            in_specs=[
                pl.BlockSpec((n_mp, tile, width), lambda i, ix: (0, i, 0)), row(feats), row(feats),
                once(n_mp, width, feats), once(n_mp, units, feats), once(n_mp, 1, units), once(n_mp, units, feats),
                once(8, feats),
            ],
            out_specs=[
                row(feats), row(feats), pl.BlockSpec((n_mp, width, tile), lambda i, ix: (0, 0, i)), row(feats), row(feats),
                row(feats), row(units), row(units), whole(8, feats),
            ],
            scratch_shapes=[pltpu.VMEM((n_mp, tile, units), bf) for _ in range(3)],
        ),
        out_shape=[
            sds((rows, feats), f32), sds((rows, feats), f32), sds((n_mp, width, rows), bf), sds((rows, feats), bf),
            sds((rows, feats), bf), sds((rows, feats), bf), sds((rows, units), bf), sds((rows, units), bf),
            sds((8, feats), f32),
        ],
        compiler_params=params(60),
        name="layer",
    )(idx, ctx, tokens, grad_out, ow, w1, b1, w2, vec)

    grad_fc2 = lax.dot_general(act_own, mix_low, (((0,), (0,)), ((), ())), preferred_element_type=f32)
    grad_fc1 = lax.dot_general(hid_low, pre_own, (((0,), (0,)), ((), ())), preferred_element_type=f32)
    ctx_own = lax.dynamic_index_in_dim(ctx, me, 0, keepdims=False)
    grad_ow = lax.dot_general(ctx_own, first_low, (((0,), (0,)), ((), ())), preferred_element_type=f32)

    input_grad, dw, dqv, dgw, dgate, acc = pl.pallas_call(
        functools.partial(attend_back_kernel, heads, hd),
        grid_spec=pltpu.PrefetchScalarGridSpec(
            num_scalar_prefetch=1,
            grid=(n_mp, seqs),
            in_specs=[
                x_spec, by_r(3 * width, feats), by_r(16, feats), by_r(heads, seq, seq), segq_spec, segk_spec, smem,
                by_rs(3 * width, seq), by_rs(width, seq), by_rs(8, seq), by_rs(8, seq),
                pl.BlockSpec((1, width, seq), lambda r, s, ix: (ix[r], 0, s)), once(rows, feats),
            ],
            out_specs=[
                whole(rows, feats), whole(3 * width, feats),
                pl.BlockSpec((1, 3 * width, seq), lambda r, s, ix: (jnp.where(r == 0, s, seqs - 1), 0, 0)),
                by_r(16, feats), by_rs(16, seq), whole(heads, seq, seq),
            ],
            scratch_shapes=[
                pltpu.VMEM((seq, seq), f32), pltpu.VMEM((2, seq, seq), f32), pltpu.VMEM((2, seq, seq), f32),
                pltpu.VMEM((2, seq, seq), bf), pltpu.VMEM((2, seq, seq), bf), pltpu.VMEM((3 * width + 16, seq), bf),
            ],
        ),
        out_shape=[
            sds((rows, feats), f32), sds((3 * width, feats), f32), sds((seqs, 3 * width, seq), bf),
            sds((n_mp, 16, feats), f32), sds((n_mp, seqs, 16, seq), f32), sds((heads, seq, seq), f32),
        ],
        compiler_params=params(60),
        name="attend_back",
    )(idx, tokens, wqkv, gsum, pos, segq, segk, scales, qkv_t, out_t, lse, gate, dctx, grad_first)

    grad_table = table_grad(buckets_t, acc, size)

    by_head = dgw[:, : 2 * heads].reshape(n_mp, 2, heads, n_mp, heads, hd)
    picked = jnp.einsum("cihcht->it", by_head)
    gate_sums = dgate.sum(axis=(1, 3))
    dbias = gate_sums[:, : 2 * heads].reshape(n_mp, 2, heads).sum(axis=(0, 2))
    dscale = lax.dynamic_index_in_dim(gate_sums, me, 0, keepdims=False)[8 : 8 + heads]
    dqv_sum = dqv.astype(f32).sum(axis=(0, 2))
    little = jnp.concatenate(
        [
            sums[:7].reshape(-1), dqv_sum[:width], dqv_sum[2 * width :], grad_table.reshape(-1), picked.reshape(-1), dbias,
            dscale,
        ]
    )
    little = lax.psum(little, "dp")
    sums = little[: 7 * feats].reshape(7, feats)
    rest = little[7 * feats :]
    dqv_bias = rest[: 2 * width].reshape(2, width)
    rest = rest[2 * width :]
    grad_table = rest[: size * heads].reshape(size, heads)
    rest = rest[size * heads :]
    grad_gate_weight = jnp.repeat(rest[: 2 * hd].reshape(2, hd), gates // 2, axis=0).T
    rest = rest[2 * hd :]
    grad_gate_bias = jnp.repeat(rest[:2], gates // 2)
    grad_gate_scale = rest[2:]

    big = jnp.concatenate([dw, grad_ow, grad_fc1, grad_fc2], axis=0).astype(bf)
    big = lax.psum(big, "dp").astype(f32)
    dw = big[: 3 * width].reshape(3, width, feats).transpose(0, 2, 1)
    grad_ow = big[3 * width : 4 * width]
    grad_fc1 = big[4 * width : 4 * width + feats]
    grad_fc2 = big[4 * width + feats :]
    return (
        normed, input_grad, dw, dqv_bias, grad_table, grad_gate_weight, grad_gate_bias, grad_gate_scale, grad_ow, sums[5],
        sums[3], sums[4], grad_fc1, sums[6], grad_fc2, sums[2], sums[0], sums[1],
    )


def solution(mesh):
    in_specs = (
        P("dp", None), P("dp", None), P(), P(None, None, "mp"), P(None, "mp"), P(None, "mp"), P(), P(), P("mp"),
        P("mp", None), P(), P(), P(), P(None, "mp"), P("mp"), P("mp", None), P(), P(), P(), P("dp", None),
    )
    out_specs = (
        P("dp", None), P("dp", None), P(None, None, "mp"), P(None, "mp"), P(None, "mp"), P(), P(), P("mp"),
        P("mp", None), P(), P(), P(), P(None, "mp"), P("mp"), P("mp", None), P(), P(), P(),
    )
    fn = functools.partial(body, mesh.shape["dp"], mesh.shape["mp"])
    return jax.shard_map(fn, mesh=mesh, in_specs=in_specs, out_specs=out_specs, check_vma=False)
```

time: 2970 us -> 454 us (0.15)
  other arithmetic: 1430 us -> 7.66 us
  local copies, waits for them, and re-layouts: 1060 us -> 29.6 us
  waiting for transfers between devices: 364 us -> 193 us
  Pallas kernels: 0 us -> 158 us
  matrix products: 55.9 us -> 4.57 us
    scatter-add x1 -> x0, other arithmetic: 1390 us -> none  [body(): jax.ops.segment_sum(table_acc.reshape(local_heads, -1).T, buckets.reshape...]
    gather x2 -> x0, local copies, waits for them, and re-layouts: 937 us -> none  [body(): pos_bias = jnp.moveaxis(rel_table[buckets], 2, 0)]
    psum x5 -> x1, waiting for transfers between devices: 364 us -> 25.3 us  [body(): big = lax.psum(big, 'dp').astype(f32)]
    all_gather x0 -> x4, waiting for transfers between devices: none -> 168 us  [gathered(): lax.all_gather(mine, ('mp', 'dp'), tiled=True)]
    pallas_call x0 -> x5, Pallas kernels: none -> 158 us  [the longest x1 49.1 us: body(): pl.pallas_call(functools.partial(attend_back_kernel, heads, hd), grid_spe...]
    transpose x5 -> x0, local copies, waits for them, and re-layouts: 58.5 us -> none  [the longest x1 58.4 us: body(): table_acc.reshape(local_heads, -1)]
    dot_general x29 -> x3, matrix products: 55.9 us -> 4.57 us  [the longest x1 1.65 us: body(): lax.dot_general(ctx_own, first_low, (((0,), (0,)), ((), ())), preferred_e...]
  transfers between devices with their start and end apart: 5 -> 5, of which waited for: 3 -> 5; matrix products, arithmetic and copies ran while one was open for 50% -> 5% of each run, Pallas kernels for 0% -> 14%
where the time goes in v1:
time: 454 us; the launch traced here: 453 us
  waiting for transfers between devices  193 us (43%)
  Pallas kernels  158 us (35%)
  blocking collectives  44.9 us (10%)
  local copies, waits for them, and re-layouts  29.6 us (7%)
  between operations  15 us (3%)
  other arithmetic  7.66 us (2%)
  matrix products  4.57 us (1%)
    all_gather x4, waiting for transfers between devices, gathered(): lax.all_gather(mine, ('mp', 'dp'), tiled=True)  168 us
    pallas_call x1, Pallas kernels, body(): pl.pallas_call(functools.partial(attend_back_kernel, heads, hd), grid_spe...  49.1 us
    pallas_call x1, Pallas kernels, body(): pl.pallas_call(layer_kernel, grid_spec=pltpu.PrefetchScalarGridSpec(num_s...  46.4 us
    pallas_call x1, Pallas kernels, body(): pl.pallas_call(functools.partial(attend_kernel, heads, hd, gates), grid_s...  27.8 us
    psum x1, waiting for transfers between devices, body(): big = lax.psum(big, 'dp').astype(f32)  25.3 us
    psum x1, blocking collectives, body(): little = lax.psum(little, 'dp')  23.7 us
    unnamed x1, blocking collectives  21.1 us
    pallas_call x1, Pallas kernels, table_grad(): pl.pallas_call(functools.partial(table_kernel, heads, tops, lows), grid=(...  17.7 us
  transfers between devices with their start and end apart: 5, of which 5 were waited for; matrix products, arithmetic and copies ran while one was open for 5% of the time, Pallas kernels for 14%

profile of v1, /device:TPU:0, one launch (start us, length us, event | category | flops | bytes accessed | tf_op | source)
XLA Modules:
  0.0 453.4 jit_solution(9171710997235923642)
XLA Ops:
  7.3 1.7 constant_dynamic-slice_fusion.4
  9.1 1.4 constant_dynamic-slice_fusion.3
  10.7 0.8 copy.99
  11.6 1.6 constant_dynamic-slice_fusion.1
  13.4 0.6 dynamic-slice.4
  14.8 0.3 dynamic-update-slice
  15.1 21.1 %all-reduce.3 = f32[8460]{0:T(1024)S(1)} all-reduce(f32[8460]{0:T(1024)S(1)} %dynamic-update-slice), channel_id=2, replica_groups=mesh['dp'=8,'mp'=4] {'mp'}, use_global_device_ids=true, to_apply=%add.3 | all-reduce | flops 8460 | bytes 67680
  36.4 0.7 slice.168.gscale_ref
  37.3 1.4 copy.86.qvb_ref
  38.8 0.6 reshape.195.table_ref
  39.4 1.3 copy.85
  41.4 0.6 broadcast_in_dim.36.segq_ref
  42.0 1.0 copy.87.segk_ref
  43.1 0.6 copy.89.b1_ref
  44.2 0.7 pad.12.gb_ref
  44.9 0.7 pad.14.gsum_ref
  45.6 17.2 %pos_bias.1 = f32[12,512,512]{2,1,0:T(8,128)} custom-call(s32[512,512]{1,0:T(8,128)} %bitcast.58, f32[12,3,128]{2,1,0:T(4,128)} %reshape.195.table_ref), custom_call_target="tpu_custom_call" | custom-call | tf_op jit(solution)/shard_map/pos_bias/pallas_call | solution.py:56
  62.7 0.6 stack.50.vec_ref
  63.4 0.5 and_select_fusion.idx_ref
  63.9 0.7 slice_reduce_fusion.4
  64.5 1.9 pad_maximum_fusion.1.gbias_ref
  66.4 8.1 %all-gather.6.cloned.1.call-done = bf16[2304,768]{1,0:T(8,128)(2,1)} async-done(((bf16[72,768]{1,0:T(8,128)(2,1)}), bf16[2304,768]{1,0:T(8,128)(2,1)}) %all-gather.6.cloned.1.call-update) | async-done | bytes 3538960 | tf_op jit(solution)/shard_map/all_gather | solution.py:377
  74.5 27.8 %attend.1 = (bf16[4,2,576,512]{3,2,1,0:T(8,128)(2,1)}, bf16[4,1024,192]{2,1,0:T(8,128)(2,1)}, f32[4,2,192,512]{3,2,1,0:T(8,128)}, f32[4,2,8,512]{3,2,1,0:T(8,128)}, f32[4,2,8,512]{3,2,1,0:T(8,128)}) custom-call(s32[4]{0:T(128)} %and_select_fusion.idx_ref, bf16[1024,768]{1,0:T(8,128)(2,1)} %x_ref.5, bf16[4,576,768]{2,1,0:T(8,128)(2,1)} %bitcast.56, ...), custom_call_target="tpu_custom_call" | custom-call | tf_op jit(solution)/shard_map/attend/pallas_call | solution.py:407
  102.4 27.9 %all-gather.8.cloned.1.call-done = bf16[768,768]{1,0:T(8,128)(2,1)} async-done(((bf16[24,768]{1,0:T(8,128)(2,1)}), bf16[768,768]{1,0:T(8,128)(2,1)}) %all-gather.8.cloned.1.call-update) | async-done | bytes 1179664 | tf_op jit(solution)/shard_map/all_gather | solution.py:377
  130.3 66.1 %all-gather.10.cloned.1.call-done = bf16[3072,768]{1,0:T(8,128)(2,1)} async-done(((bf16[96,768]{1,0:T(8,128)(2,1)}), bf16[3072,768]{1,0:T(8,128)(2,1)}) %all-gather.10.cloned.1.call-update) | async-done | bytes 4718608 | tf_op jit(solution)/shard_map/all_gather | solution.py:377
  196.4 65.8 %all-gather.12.cloned.1.call-done = bf16[3072,768]{1,0:T(8,128)(2,1)} async-done(((bf16[96,768]{1,0:T(8,128)(2,1)}), bf16[3072,768]{1,0:T(8,128)(2,1)}) %all-gather.12.cloned.1.call-update) | async-done | bytes 4718608 | tf_op jit(solution)/shard_map/all_gather | solution.py:377
  262.2 46.4 %layer.1 = (f32[1024,768]{1,0:T(8,128)}, f32[1024,768]{1,0:T(8,128)}, bf16[4,192,1024]{2,1,0:T(8,128)(2,1)}, bf16[1024,768]{1,0:T(8,128)(2,1)}, bf16[1024,768]{1...) custom-call(s32[4]{0:T(128)} %and_select_fusion.idx_ref, ...), custom_call_target="tpu_custom_call" | custom-call | tf_op jit(solution)/shard_map/layer/pallas_call | solution.py:437
  308.6 49.1 %attend_back.1 = (f32[1024,768]{1,0:T(8,128)}, f32[576,768]{1,0:T(8,128)}, bf16[2,576,512]{2,1,0:T(8,128)(2,1)}, f32[4,16,768]{2,1,0:T(8,128)}, f32[4,2,16,512]{3,2,1,0:T(8,128)}, /*index=5*/f32[3,512,512]{2,1,0:T(8,128)}) custom-call(s32[4]{0:T(128)} %and_select_fusion.idx_ref, bf16[1024,768]{1,0:T(8,128)(2,1)} %x_ref.5, bf16[4,576,768]{2,1,0:T(8,128)(2,1)} %bitcast.57, ...), custom_call_target="tpu_custom_call" | custom-call | tf_op jit(solution)/shard_map/attend_back/pallas_call | solution.py:467
  357.7 1.7 convert.23
  359.6 1.7 convolution_convert_fusion.2
  361.3 1.5 convolution_convert_fusion.1
  362.8 0.4 copy-done.23
  363.2 1.5 convolution_convert_fusion
  364.7 2.1 pad_maximum_fusion
  367.0 17.7 %table_grad.1 = f32[24,48]{1,0:T(8,128)} custom-call(s32[512,512]{1,0:T(8,128)} %bitcast.59, f32[3,512,512]{2,1,0:T(8,128)} %get-tuple-element.55.val_ref), custom_call_target="tpu_custom_call" | custom-call | tf_op jit(solution)/shard_map/table_grad/pallas_call | solution.py:332
  384.7 0.8 copy.92
  386.7 0.2 convert_reduce_fusion
  387.1 23.7 %psum.15 = f32[6853]{0:T(1024)S(1)} all-reduce(f32[6853]{0:T(1024)S(1)} %concatenate.21), channel_id=1, replica_groups=mesh['dp'=8,'mp'=4] {'dp'}, use_global_device_ids=true, to_apply=%region_12.13 | all-reduce | flops 6853 | bytes 54824 | tf_op jit(solution)/shard_map/psum | solution.py:509
  411.0 0.6 slice.176
  411.7 0.7 copy.95
  412.5 0.7 reshape.206
  413.3 0.6 reshape.210
  413.8 0.6 fusion.6
  414.5 25.3 %all-reduce.6.cloned.1.call-done = bf16[2304,768]{1,0:T(8,128)(2,1)} async-done(((bf16[2304,768]{1,0:T(8,128)(2,1)}), bf16[2304,768]{1,0:T(8,128)(2,1)}) %all-reduce.6.cloned.1.call-update) | async-done | bytes 3538960 | tf_op jit(solution)/shard_map/psum | solution.py:522
  439.8 4.3 fusion.5
  444.1 1.3 slice.170
  445.4 0.9 slice.177
  446.3 0.6 broadcast_in_dim.44
  (129 shorter events, 4.4 us)
Async XLA Ops:
  7.2 3.4 copy-start
  7.2 6.2 %copy-start.26 = (u32[32]{0:T(128)S(1)}, u32[32]{0:T(128)}, u32[]{:S(2)}) copy-start(u32[32]{0:T(128)} %constant.68) | copy-start | bytes 388
  7.2 6.0 %copy-start.11 = (f32[320,3]{0,1:T(4,128)S(1)}, f32[320,3]{0,1:T(4,128)}, u32[]{:S(2)}) copy-start(f32[320,3]{0,1:T(4,128)} %param.25) | copy-start | bytes 11524
  7.2 6.1 %copy-start.19 = (f32[2,192]{1,0:T(2,128)S(1)}, f32[2,192]{1,0:T(2,128)}, u32[]{:S(2)}) copy-start(f32[2,192]{1,0:T(2,128)} %param.24) | copy-start | bytes 4612
  7.2 7.4 %copy-start.21 = (f32[3]{0:T(128)S(1)}, f32[3]{0:T(128)}, u32[]{:S(2)}) copy-start(f32[3]{0:T(128)} %param.28) | copy-start | bytes 40
  7.3 7.4 %copy-start.18 = (f32[768]{0:T(1024)S(1)}, f32[768]{0:T(1024)}, u32[]{:S(2)}) copy-start(f32[768]{0:T(1024)} %param.34) | copy-start | bytes 9220
  7.3 67.3 %all-gather.6.cloned.1.call-start = ((), (), s32[]{:S(2)}) async-start(), calls=%async_computation | async-start | bytes 3649536 | tf_op jit(solution)/shard_map/all_gather | solution.py:377
  7.3 32.1 %copy-start.5 = (s32[512,512]{1,0:T(8,128)S(1)}, s32[512,512]{1,0:T(8,128)}, u32[]{:S(2)}) copy-start(s32[512,512]{1,0:T(8,128)} %param.22) | copy-start | bytes 3145732
  9.0 121.3 %all-gather.8.cloned.1.call-start = ((), (), s32[]{:S(2)}) async-start(), calls=%async_computation.1 | async-start | bytes 1216512 | tf_op jit(solution)/shard_map/all_gather | solution.py:377
  10.5 185.9 %all-gather.10.cloned.1.call-start = ((), (), s32[]{:S(2)}) async-start(), calls=%async_computation.2 | async-start | bytes 4866048 | tf_op jit(solution)/shard_map/all_gather | solution.py:377
  11.5 250.7 %all-gather.12.cloned.1.call-start = ((), (), s32[]{:S(2)}) async-start(), calls=%async_computation.3 | async-start | bytes 4866048 | tf_op jit(solution)/shard_map/all_gather | solution.py:377
  13.2 426.6 %all-reduce.6.cloned.1.call-start = ((), (), s32[]{:S(2)}) async-start(), calls=%async_computation.4 | async-start | bytes 7077888 | tf_op jit(solution)/shard_map/psum | solution.py:522
  38.7 2.5 copy-start.10
  38.7 2.7 copy-start.9
  39.4 4.3 copy-start.12
  39.4 4.3 copy-start.13
  39.4 4.3 copy-start.14
  39.4 4.3 copy-start.15
  39.4 4.3 copy-start.16
  39.4 4.3 copy-start.17
  45.6 18.3 %copy-start.20 = (f32[8]{0:T(128)S(1)}, f32[8]{0:T(128)}, u32[]{:S(2)}) copy-start(f32[8]{0:T(128)} %param.27) | copy-start | bytes 100
  357.7 1.9 copy-start.3
  357.7 3.6 copy-start.25
  359.4 1.9 copy-start.24
  361.3 1.5 copy-start.22
  361.3 1.9 copy-start.23
  367.0 19.0 %copy-start.7 = (f32[4,16,768]{2,1,0:T(8,128)S(1)}, f32[4,16,768]{2,1,0:T(8,128)}, u32[]{:S(2)}) copy-start(f32[4,16,768]{2,1,0:T(8,128)} %get-tuple-element.56) | copy-start | bytes 589828
  367.0 19.3 %copy-start.6 = (f32[4,2,16,512]{3,2,1,0:T(8,128)S(1)}, f32[4,2,16,512]{3,2,1,0:T(8,128)}, u32[]{:S(2)}) copy-start(f32[4,2,16,512]{3,2,1,0:T(8,128)} %get-tuple-element.57) | copy-start | bytes 786436
  367.0 19.6 %copy-start.8 = (f32[8,768]{1,0:T(8,128)S(1)}, f32[8,768]{1,0:T(8,128)}, u32[]{:S(2)}) copy-start(f32[8,768]{1,0:T(8,128)} %get-tuple-element.53) | copy-start | bytes 73732
  367.0 19.7 %copy-start.4 = (bf16[2,576,512]{2,1,0:T(8,128)(2,1)S(1)}, bf16[2,576,512]{2,1,0:T(8,128)(2,1)}, u32[]{:S(2)}) copy-start(bf16[2,576,512]{2,1,0:T(8,128)(2,1)} %get-tuple-element.54) | copy-start | bytes 3538948
  439.8 4.3 copy-start.2
  439.8 7.1 %copy-start.1 = (bf16[768,768]{1,0:T(8,128)(2,1)S(1)}, bf16[768,768]{1,0:T(8,128)(2,1)}, u32[]{:S(2)}) copy-start(bf16[768,768]{1,0:T(8,128)(2,1)} %param.33) | copy-start | bytes 3538948
Sparse Core Ops, SparseCore 0:
  11.6 62.9 all-gather.5
  77.4 52.8 all-gather.7
  133.8 62.5 all-gather.9
  199.7 62.4 all-gather.11
  366.9 72.8 all-reduce.5

commit v2 on v1

v2 whole, which is shorter than its diff:
```python
import functools

import jax
import jax.numpy as jnp
from jax import lax
from jax.experimental import pallas as pl
from jax.experimental.pallas import tpu as pltpu
from jax.sharding import PartitionSpec as P

norm_eps = 1e-05
deep_alpha = 24.0**0.25
masked_score = -1e30
bf = jnp.bfloat16
f32 = jnp.float32
LANES = 128
LIMIT = 60
COST = 3_000_000_000


def nn(a, b):
    return lax.dot_general(a, b, (((1,), (0,)), ((), ())), preferred_element_type=f32)


def nt(a, b):
    return lax.dot_general(a, b, (((1,), (1,)), ((), ())), preferred_element_type=f32)


def params(mib):
    return pltpu.CompilerParams(vmem_limit_bytes=mib * 1024 * 1024)


def lines_kernel(table_ref, b1_ref, qv_ref, scale_ref, out_ref, cut_ref):
    heads, size = table_ref.shape
    feats = out_ref.shape[1]
    width = qv_ref.shape[1]
    out_ref[...] = jnp.zeros_like(out_ref)
    per = -(-size // LANES) * LANES
    for h in range(heads):
        out_ref[pl.ds(h * per // feats, 1), pl.ds(h * per % feats, size)] = table_ref[pl.ds(h, 1), :]
    out_ref[pl.ds(2, 1), :] = b1_ref[...]
    out_ref[pl.ds(3, 1), pl.ds(0, width)] = qv_ref[pl.ds(0, 1), :]
    out_ref[pl.ds(3, 1), pl.ds(256, width)] = qv_ref[pl.ds(1, 1), :]
    out_ref[pl.ds(3, 1), pl.ds(512, heads)] = scale_ref[...]
    rest = out_ref[...]
    cuts = []
    for _ in range(3):
        cut = rest.astype(bf).astype(f32)
        cuts.append(cut)
        rest = rest - cut
    cut_ref[...] = jnp.concatenate(cuts + [jnp.zeros_like(rest)], axis=0).astype(bf)


def lines_of(table, b1, qv, scale):
    feats = b1.shape[1]
    return pl.pallas_call(
        lines_kernel,
        out_shape=[jax.ShapeDtypeStruct((4, feats), f32), jax.ShapeDtypeStruct((16, feats), bf)],
        compiler_params=params(LIMIT),
        name="lines",
    )(table, b1, qv, scale)


def bias_kernel(heads, chunks, buckets_ref, small_ref, out_ref):
    rows, cols = buckets_ref.shape
    groups, _, feats = small_ref.shape
    for r in range(0, rows, 8):
        at = pl.ds(r, 8)
        for c in range(cols // LANES):
            lanes = pl.ds(c * LANES, LANES)
            idx = buckets_ref[at, lanes]
            low = idx & (LANES - 1)
            high = idx >> 7
            for h in range(heads):
                got = None
                for k in range(chunks):
                    spot = ((h % 3) * chunks + k) * LANES
                    line = jnp.broadcast_to(
                        small_ref[h // 3, pl.ds(spot // feats, 1), pl.ds(spot % feats, LANES)], (8, LANES)
                    )
                    part = jnp.take_along_axis(line, low, axis=1, mode="promise_in_bounds")
                    got = part if got is None else jnp.where(high == k, part, got)
                out_ref[h, at, lanes] = got


def bias_of(buckets_t, small, heads, size):
    groups, _, feats = small.shape
    seq = buckets_t.shape[0]
    rows = 64
    cost = pl.CostEstimate(flops=COST, bytes_accessed=1 << 20, transcendentals=0)
    return pl.pallas_call(
        functools.partial(bias_kernel, heads * groups, -(-size // LANES)),
        grid=(seq // rows,),
        in_specs=[
            pl.BlockSpec((rows, seq), lambda i: (i, 0)),
            pl.BlockSpec((groups, 4, feats), lambda i: (0, 0, 0)),
        ],
        out_specs=pl.BlockSpec((heads * groups, rows, seq), lambda i: (0, i, 0)),
        out_shape=jax.ShapeDtypeStruct((heads * groups, seq, seq), f32),
        compiler_params=params(LIMIT),
        cost_estimate=cost,
        name="pos_bias",
    )(buckets_t, small)


def head_lanes(shape, head, hd):
    return lax.broadcasted_iota(jnp.int32, shape, 1) // hd == head


def fill_mask(mask, segq_ref, segk_ref, row):
    seq = mask.shape[0]
    for c in range(seq // LANES):
        lanes = pl.ds(c * LANES, LANES)
        mask[:, lanes] = jnp.where(segk_ref[row] == segq_ref[row, :, lanes], 0.0, masked_score)


def attend_kernel(
    heads, hd, group, x_hbm, wt_hbm, wl_hbm, pos_hbm, gw_ref, small_ref, segq_ref, segk_ref, gbias_ref, at_ref,
    qkv_hbm, ctx_hbm, out_hbm, lse_ref, gate_ref,
    x_v, w_v, pos_v, qkv_v, ctx_v, out_v, mask, sc, pr, sem,
):
    width = heads * hd
    seqs, _, seq = segq_ref.shape
    gates = gw_ref.shape[0]
    half = gates // 2
    cut = wt_hbm.shape[1]

    def line(row):
        return pl.ds(row * seq, seq)

    copy = pltpu.make_async_copy
    x_in = [copy(x_hbm.at[line(r)], x_v.at[r], sem.at[r]) for r in range(seqs)]
    w_in = [
        copy(wt_hbm.at[group], w_v.at[pl.ds(0, cut)], sem.at[seqs]),
        copy(wl_hbm.at[group, pl.ds(0, 3 * width - cut)], w_v.at[pl.ds(cut, 3 * width - cut)], sem.at[seqs + 1]),
    ]
    pos_in = [copy(pos_hbm.at[group * heads + h], pos_v.at[h], sem.at[seqs + 2 + h]) for h in range(heads)]
    base = seqs + 2 + heads
    out_copies = [
        [copy(qkv_v.at[r], qkv_hbm.at[r], sem.at[base + 3 * r]), copy(ctx_v.at[line(r)], ctx_hbm.at[line(r)], sem.at[base + 3 * r + 1]),
         copy(out_v.at[r], out_hbm.at[r], sem.at[base + 3 * r + 2])]
        for r in range(seqs)
    ]
    for c in [x_in[0]] + w_in + [pos_in[0]] + x_in[1:] + pos_in[1:]:
        c.start()

    cols = jnp.broadcast_to(small_ref[group, pl.ds(3, 1), pl.ds(0, 512)], (8, 512)).T[:, :1]
    gw = gw_ref[...].astype(f32)
    mine = [jnp.where(head_lanes(gw.shape, at_ref[0] * heads + h, hd), gw, 0.0) for h in range(heads)]
    mine = jnp.concatenate(mine, axis=0).astype(bf)
    bias_a = gbias_ref[0] + gbias_ref[1] + gbias_ref[2] + gbias_ref[3]
    bias_b = gbias_ref[4] + gbias_ref[5] + gbias_ref[6] + gbias_ref[7]
    lins = {}

    def project(row):
        x_in[row].wait()
        if row == 0:
            for c in w_in:
                c.wait()
        x = x_v[row]
        both = nt(w_v[...], x)
        qkv_v[row, pl.ds(0, width), :] = (both[:width] + cols[:width]).astype(bf) * bf(hd**-0.5)
        qkv_v[row, pl.ds(width, width), :] = both[width : 2 * width].astype(bf)
        qkv_v[row, pl.ds(2 * width, width), :] = (both[2 * width :] + cols[256 : 256 + width]).astype(bf)
        lins[row] = nt(mine, x)
        fill_mask(mask.at[row], segq_ref, segk_ref, row)
        out_copies[row][0].start()

    def score(i):
        row, h = divmod(i, heads)
        k_t = qkv_v[row, pl.ds(width + h * hd, hd), :]
        sc[i % 2] = nn(k_t.T, qkv_v[row, pl.ds(h * hd, hd), :])

    def weigh(i):
        row, h = divmod(i, heads)
        if row == 0:
            pos_in[h].wait()
        lin = lins[row]
        first = jax.nn.sigmoid(jnp.sum(lin[h * gates : h * gates + half], axis=0, keepdims=True) + bias_a)
        second = jax.nn.sigmoid(jnp.sum(lin[h * gates + half : (h + 1) * gates], axis=0, keepdims=True) + bias_b)
        gate = first * (second * small_ref[group, pl.ds(3, 1), pl.ds(512 + h, 1)] - 1.0) + 2.0
        gate_ref[row, pl.ds(h, 1), :] = first
        gate_ref[row, pl.ds(heads + h, 1), :] = second
        for c in range(seq // LANES):
            lanes = pl.ds(c * LANES, LANES)
            s = sc[i % 2, :, lanes] + pos_v[h, :, lanes] * gate[:, c * LANES : (c + 1) * LANES] + mask[row, :, lanes]
            top = jnp.max(s, axis=0, keepdims=True)
            p = jnp.exp(s - top)
            total = jnp.sum(p, axis=0, keepdims=True)
            pr[i % 2, :, lanes] = p.astype(bf)
            lse_ref[row, pl.ds(h, 1), lanes] = top + jnp.log(total)
            lse_ref[row, pl.ds(heads + h, 1), lanes] = 1.0 / total

    def gather(i):
        row, h = divmod(i, heads)
        v_t = qkv_v[row, pl.ds(2 * width + h * hd, hd), :]
        out_v[row, pl.ds(h * hd, hd), :] = nn(v_t, pr[i % 2]) * lse_ref[row, pl.ds(heads + h, 1), :]
        if h == heads - 1:
            out_copies[row][2].start()
            ctx_v[line(row), :] = out_v[row].T.astype(bf)
            out_copies[row][1].start()

    count = seqs * heads
    project(0)
    score(0)
    for i in range(count):
        if i + 1 < count:
            if (i + 1) % heads == 0:
                project((i + 1) // heads)
            score(i + 1)
        weigh(i)
        if i:
            gather(i - 1)
    gather(count - 1)
    for row in out_copies:
        for c in row:
            c.wait()


def attend_back_kernel(
    heads, hd, which, wt_hbm, wl_hbm, pos_hbm, qkv_hbm, out_hbm, dctx_hbm, base_hbm, x_hbm,
    gw_ref, small_ref, segq_ref, segk_ref, at_ref, lse_ref, gate_ref, *rest,
):
    own, group = which == 0, max(which - 1, 0)
    if own:
        grad_hbm, dw_hbm, tiny_ref, table_hbm = rest[:4]
        dw_v, x_v, parts, table_v, table_sem = rest[-5:]
        rest = rest[4:-5]
    else:
        grad_hbm = rest[0]
        rest = rest[1:]
    w_v, pos_v, qkv_v, out_v, dctx_v, base_v, mask, sc, dp, pr, ds, wide, sem = rest
    width = heads * hd
    seqs, _, seq = segq_ref.shape
    feats = w_v.shape[1]
    cut = wt_hbm.shape[1]

    def line(row):
        return pl.ds(row * seq, seq)

    copy = pltpu.make_async_copy
    w_in = [
        copy(wt_hbm.at[group], w_v.at[pl.ds(0, cut)], sem.at[0]),
        copy(wl_hbm.at[group, pl.ds(0, 3 * width - cut)], w_v.at[pl.ds(cut, 3 * width - cut)], sem.at[1]),
    ]
    pos_in = [copy(pos_hbm.at[group * heads + h], pos_v.at[h], sem.at[2 + h]) for h in range(heads)]
    spot = 2 + heads
    row_in, base_in, grad_out = [], [], []
    for r in range(seqs):
        row_in.append([
            copy(qkv_hbm.at[r], qkv_v.at[r], sem.at[spot]), copy(dctx_hbm.at[which, r], dctx_v.at[r], sem.at[spot + 1]),
            copy(out_hbm.at[r], out_v.at[r], sem.at[spot + 2]),
        ])
        base_in.append(copy(base_hbm.at[line(r)], base_v.at[r], sem.at[spot + 3]))
        grad_out.append(copy(base_v.at[r], grad_hbm.at[line(r)], sem.at[spot + 4]))
        spot += 5
    for c in row_in[0] + [pos_in[0]] + row_in[1] + pos_in[1:] + w_in + base_in:
        c.start()
    if own:
        x_in = [copy(x_hbm.at[line(r)], x_v.at[r], table_sem.at[heads + 1 + r]) for r in range(seqs)]
        table_out = [copy(table_v.at[h], table_hbm.at[h], table_sem.at[h]) for h in range(heads)]
        dw_out = copy(dw_v, dw_hbm, table_sem.at[heads])
        for c in x_in:
            c.start()

    gw = gw_ref[...].astype(f32)
    half = gw.shape[0] // 2
    sums = [jnp.sum(gw[:half], axis=0, keepdims=True), jnp.sum(gw[half:], axis=0, keepdims=True)]
    lanes_of = [head_lanes((1, feats), at_ref[0] * heads + h, hd) for h in range(heads)]
    gsum = [jnp.where(lanes_of[h], part, 0.0) for part in sums for h in range(heads)]
    w_v[pl.ds(3 * width, 16), :] = jnp.concatenate(gsum + [jnp.zeros((16 - 2 * heads, feats), f32)], axis=0).astype(bf)
    gate_parts = {}

    def score(i):
        row, h = divmod(i, heads)
        if h == 0:
            for c in row_in[row]:
                c.wait()
            fill_mask(mask.at[row], segq_ref, segk_ref, row)
        k_t = qkv_v[row, pl.ds(width + h * hd, hd), :]
        v_t = qkv_v[row, pl.ds(2 * width + h * hd, hd), :]
        sc[i % 2] = nn(k_t.T, qkv_v[row, pl.ds(h * hd, hd), :])
        dp[i % 2] = nn(v_t.T, dctx_v[row, pl.ds(h * hd, hd), :])

    def weigh(i):
        row, h = divmod(i, heads)
        if row == 0:
            pos_in[h].wait()
        b = i % 2
        g_t = dctx_v[row, pl.ds(h * hd, hd), :]
        first = gate_ref[row, pl.ds(h, 1), :]
        second = gate_ref[row, pl.ds(heads + h, 1), :]
        scale = small_ref[group, pl.ds(3, 1), pl.ds(512 + h, 1)]
        gate = first * (second * scale - 1.0) + 2.0
        centre = jnp.sum(g_t.astype(f32) * out_v[row, pl.ds(h * hd, hd), :], axis=0, keepdims=True)
        lse = lse_ref[row, pl.ds(h, 1), :]
        sums_of = []
        for c in range(seq // LANES):
            lanes = pl.ds(c * LANES, LANES)
            at = slice(c * LANES, (c + 1) * LANES)
            pos = pos_v[h, :, lanes]
            p = jnp.exp(sc[b, :, lanes] + (pos * gate[:, at] - lse[:, at]) + mask[row, :, lanes])
            pr[b, :, lanes] = p.astype(bf)
            d = p * (dp[b, :, lanes] - centre[:, at])
            ds[b, :, lanes] = d.astype(bf)
            sums_of.append(jnp.sum(d * pos, axis=0, keepdims=True))
            if own:
                tab = gate[:, at] * d
                if row == 0:
                    table_v[h, :, lanes] = tab
                else:
                    table_v[h, :, lanes] += tab
        if own and row == seqs - 1:
            table_out[h].start()
        dgate = jnp.concatenate(sums_of, axis=1)
        dfirst = dgate * (second * scale - 1.0) * first * (1.0 - first)
        dsecond = dgate * first * scale * second * (1.0 - second)
        gate_parts[i] = (dfirst, dsecond, dgate * first * second)

    def gather(i):
        row, h = divmod(i, heads)
        b = i % 2
        q_t = qkv_v[row, pl.ds(h * hd, hd), :]
        k_t = qkv_v[row, pl.ds(width + h * hd, hd), :]
        g_t = dctx_v[row, pl.ds(h * hd, hd), :]
        for j, d in enumerate((nn(k_t, ds[b]) * hd**-0.5, nt(q_t, ds[b]), nt(g_t, pr[b]))):
            hi = d.astype(bf)
            wide[row, pl.ds(j * width + h * hd, hd), :] = hi
            if own:
                parts[row, pl.ds(j * width + h * hd, hd), :] = (d - hi.astype(f32)).astype(bf)
        if h < heads - 1:
            return
        lines = [gate_parts[row * heads + j][k] for k in (0, 1) for j in range(heads)]
        low = jnp.concatenate(lines + [jnp.zeros((16 - 2 * heads, seq), f32)], axis=0).astype(bf)
        wide[row, pl.ds(3 * width, 16), :] = low
        if row == 0:
            for c in w_in:
                c.wait()
        part = nn(wide[row].T, w_v[...])
        base_in[row].wait()
        base_v[row] = deep_alpha * base_v[row] + part if own else base_v[row] + part
        grad_out[row].start()
        if not own:
            return
        x_in[row].wait()
        x = x_v[row]
        main = wide[row, pl.ds(0, 3 * width), :]
        dw_here = nn(main, x) + nn(parts[row], x)
        dgw = nn(low, x)
        one = sum(jnp.where(lanes_of[j], dgw[j : j + 1], 0.0) for j in range(heads))
        two = sum(jnp.where(lanes_of[j], dgw[heads + j : heads + j + 1], 0.0) for j in range(heads))
        qv = nt(jnp.ones((8, seq), bf), main)[:1]
        lane = lax.broadcasted_iota(jnp.int32, (1, feats), 1)

        def spot_of(k, v):
            return jnp.where(lane == k, jnp.sum(v, axis=1, keepdims=True), 0.0)

        biases = spot_of(0, sum(lines[:heads])) + spot_of(1, sum(lines[heads:]))
        gains = sum(spot_of(j, gate_parts[row * heads + j][2]) for j in range(heads))
        none = jnp.zeros((1, feats), f32)
        qv = jnp.concatenate([qv, none[:, : feats - qv.shape[1]]], axis=1)
        here = jnp.concatenate([one, two, biases, none, qv, gains, none, none], axis=0)
        if row == 0:
            dw_v[...] = dw_here
            tiny_ref[...] = here
        else:
            dw_v[...] += dw_here
            tiny_ref[...] += here
        if row == seqs - 1:
            dw_out.start()

    count = seqs * heads
    score(0)
    for i in range(count):
        if i + 1 < count:
            score(i + 1)
        weigh(i)
        if i:
            gather(i - 1)
    gather(count - 1)
    for c in grad_out:
        c.wait()
    if own:
        for c in table_out + [dw_out]:
            c.wait()


def norm_stats(v):
    mean = jnp.mean(v, axis=-1, keepdims=True)
    cen = v - mean
    rs = lax.rsqrt(jnp.mean(cen * cen, axis=-1, keepdims=True) + norm_eps)
    return cen * rs, rs


def norm_back(g, n, rs, gain):
    gn = g * gain
    return rs * (gn - jnp.mean(gn, axis=-1, keepdims=True) - n * jnp.mean(gn * n, axis=-1, keepdims=True))


def gelu_pair(x):
    cdf = 0.5 + 0.5 * lax.erf(x * 0.5**0.5)
    return x * cdf, cdf + x * jnp.exp(x * x * -0.5) * 0.3989422804014327


def layer_kernel(
    ctx0_ref, ctx1_ref, ctx2_ref, ctx3_ref, x_ref, go_ref, ow0_hbm, ow_hbm, w10_hbm, w1a_hbm, w1b_hbm, small_ref, b1a_ref, b1b_ref,
    w20_hbm, w2a_hbm, w2b_hbm, vec_ref, at_ref,
    out_ref, first_ref, dctx_ref, hid_low_ref, mix_low_ref, first_low_ref, act_ref, pre_low_ref, sums_ref,
    ow_v, w1_v, w2_v, act, slope, plow, sem,
):
    step = pl.program_id(0)
    ctxs = (ctx0_ref, ctx1_ref, ctx2_ref, ctx3_ref)
    width = ow0_hbm.shape[0]
    own = w10_hbm.shape[0]
    half = w1a_hbm.shape[0]
    part = w2a_hbm.shape[1]
    copy = pltpu.make_async_copy
    ow_in = [copy(ow0_hbm, ow_v.at[pl.ds(0, width)], sem.at[0])]
    for i in range(1, len(ctxs)):
        ow_in.append(copy(ow_hbm.at[i - 1, pl.ds(ow_hbm.shape[1] - width, width)], ow_v.at[pl.ds(i * width, width)], sem.at[i]))
    w1_in = [
        copy(w10_hbm, w1_v.at[pl.ds(0, own)], sem.at[4]),
        copy(w1a_hbm, w1_v.at[pl.ds(own, half)], sem.at[5]),
        copy(w1b_hbm, w1_v.at[pl.ds(own + half, half)], sem.at[6]),
    ]
    w2_in = [copy(w20_hbm, w2_v.at[pl.ds(0, own)], sem.at[7])]
    for i in range(1, len(ctxs)):
        for k, src in enumerate((w2a_hbm, w2b_hbm)):
            spot = pl.ds(own + k * half + (i - 1) * part, part)
            w2_in.append(copy(src.at[at_ref[i]], w2_v.at[spot], sem.at[6 + 2 * i + k]))

    @pl.when(step == 0)
    def _():
        for c in ow_in + w1_in + w2_in:
            c.start()
        for c in ow_in:
            c.wait()

    vec = vec_ref[...]
    out_bias, gain1, bias1, bias2, gain2, beta2 = (vec[i : i + 1] for i in range(6))
    total = deep_alpha * x_ref[...].astype(f32) + out_bias
    for i, c in enumerate(ctxs):
        total = total + nn(c[...], ow_v[pl.ds(i * width, width), :])
    n1, rs1 = norm_stats(total)
    hidden = n1 * gain1 + bias1
    hid_low = hidden.astype(bf)
    hid_low_ref[...] = hid_low

    @pl.when(step == 0)
    def _():
        for c in w1_in:
            c.wait()

    block = 256
    b1 = jnp.concatenate(
        [small_ref[pl.ds(2, 1), :]] + [ref[pl.ds(i, 1), :] for ref in (b1a_ref, b1b_ref) for i in range(len(ctxs) - 1)], axis=1
    )
    blocks = [pl.ds(u, block) for u in range(0, w1_v.shape[0], block)]
    for at in blocks:
        pre = nt(hid_low, w1_v[at, :]) + b1[:, at.start : at.start + block]
        a, s = gelu_pair(pre)
        act[:, at] = a.astype(bf)
        slope[:, at] = s

    @pl.when(step == 0)
    def _():
        for c in w2_in:
            c.wait()

    mixed = deep_alpha * hidden + bias2 + nn(act[...], w2_v[...])
    act_ref[...] = act[:, pl.ds(0, own)]
    n2, rs2 = norm_stats(mixed)
    out_ref[...] = n2 * gain2 + beta2
    g = go_ref[...].astype(f32)
    grad_mixed = norm_back(g, n2, rs2, gain2)
    mix_low = grad_mixed.astype(bf)
    mix_low_ref[...] = mix_low
    line = []
    for at in blocks:
        d = nt(mix_low, w2_v[at, :]) * slope[:, at]
        if at.start < own:
            line.append(jnp.sum(d, axis=0, keepdims=True))
        plow[:, at] = d.astype(bf)
    b1_sum = jnp.concatenate(line, axis=1)
    grad_hidden = deep_alpha * grad_mixed + nn(plow[...], w1_v[...])
    pre_low_ref[...] = plow[:, pl.ds(0, own)]
    grad_first = norm_back(grad_hidden, n1, rs1, gain1)
    first_ref[...] = grad_first
    first_low = grad_first.astype(bf)
    first_low_ref[...] = first_low
    first_rest = (grad_first - first_low.astype(f32)).astype(bf)
    dctx = (nt(ow_v[...], first_low) + nt(ow_v[...], first_rest)).astype(bf)
    for i in range(len(ctxs)):
        dctx_ref[i, 0] = dctx[i * width : (i + 1) * width]

    def col(v):
        return jnp.sum(v, axis=0, keepdims=True)

    sums = jnp.concatenate(
        [
            col(g * n2), col(g), col(grad_mixed), col(grad_hidden * n1), col(grad_hidden), col(grad_first), b1_sum,
            jnp.zeros_like(b1_sum),
        ],
        axis=0,
    )

    @pl.when(step == 0)
    def _():
        sums_ref[...] = sums

    @pl.when(step != 0)
    def _():
        sums_ref[...] += sums


def table_kernel(heads, tops, lows, buckets_ref, val_ref, out_ref):
    rows, cols = buckets_ref.shape
    top_id = lax.broadcasted_iota(jnp.int32, (tops, cols), 0)
    low_id = lax.broadcasted_iota(jnp.int32, (lows, cols), 0)
    unroll = 32

    def group(g, acc):
        for u in range(0, unroll, 8):
            at = pl.ds(pl.multiple_of(g * unroll, unroll) + u, 8)
            idx = buckets_ref[at, :]
            high = idx >> 4
            low = idx & 15
            vals = [val_ref[h, at, :] for h in range(heads)]
            for i in range(8):
                a = jnp.where(high[i : i + 1] == top_id, 1.0, 0.0).astype(bf)
                hit = low[i : i + 1] == low_id
                b = jnp.concatenate([jnp.where(hit, v[i : i + 1], 0.0).astype(bf) for v in vals], axis=0)
                acc = acc + nt(a, b)
        return acc

    out_ref[...] = lax.fori_loop(0, rows // unroll, group, jnp.zeros(out_ref.shape, f32))


def table_grad(buckets_t, values, size):
    heads, seq, _ = values.shape
    lows = 16
    tops = -(-size // lows // 8) * 8
    return pl.pallas_call(
        functools.partial(table_kernel, heads, tops, lows),
        out_shape=jax.ShapeDtypeStruct((tops, heads * lows), f32),
        compiler_params=params(LIMIT),
        cost_estimate=pl.CostEstimate(flops=COST, bytes_accessed=1 << 20, transcendentals=0),
        name="table_grad",
    )(buckets_t, values)


def rotate(x, by, n):
    return lax.ppermute(x, "mp", [(i, (i + by) % n) for i in range(n)])


def swap(x, bit, n, axis="dp"):
    return lax.ppermute(x, axis, [(i, i ^ bit) for i in range(n)])


def after(x, *earlier):
    return lax.optimization_barrier((x,) + earlier)[0]


def joined(pieces, got, bit, index, have):
    at = 1 + sum(b > bit for b in have)
    mine = (index & bit) != 0
    return jnp.stack([jnp.where(mine, got, pieces), jnp.where(mine, pieces, got)], axis=at)


def body(
    n_dp, n_mp,
    tokens, segment_ids, buckets, qkv_weight, qv_bias, rel_table, gate_weight, gate_bias, gate_scale, out_weight,
    out_bias, ln1_gain, ln1_bias, fc1_weight, fc1_bias, fc2_weight, fc2_bias, ln2_gain, ln2_bias, grad_out,
):
    rows, feats = tokens.shape
    seqs, seq = segment_ids.shape
    size, heads = rel_table.shape
    hd, gates = gate_weight.shape
    width = heads * hd
    units = fc1_weight.shape[1]
    me = lax.axis_index("mp")
    dp = lax.axis_index("dp")
    order = ((me - jnp.arange(n_mp)) % n_mp).astype(jnp.int32)
    bits = [1 << i for i in range(n_dp.bit_length() - 1)]
    plane = bits[1:]
    others = n_mp - 1
    core = dp & 1
    sds = jax.ShapeDtypeStruct

    hbm = pl.BlockSpec(memory_space=pl.ANY)
    smem = pl.BlockSpec(memory_space=pltpu.SMEM)
    full = pl.BlockSpec()
    square = pltpu.VMEM((seqs, seq, seq), f32)
    pair = pltpu.VMEM((2, seq, seq), f32)
    low_pair = pltpu.VMEM((2, seq, seq), bf)
    segq = segment_ids[:, None, :]
    segk = segment_ids[:, :, None]
    gw = jnp.tile(gate_weight.T, (1, n_mp * heads))
    lines_t = pltpu.VMEM((seqs, 3 * width, seq), bf)
    outs_t = pltpu.VMEM((seqs, width, seq), f32)
    tables_t = pltpu.VMEM((heads, seq, seq), f32)

    def attend(i, sources, *deps):
        wt, wl, sm, pos = sources
        return pl.pallas_call(
            functools.partial(attend_kernel, heads, hd, max(i - 1, 0)),
            in_specs=[hbm] * 4 + [full] * 4 + [smem] * 2,
            out_specs=[hbm] * 3 + [full] * 2,
            scratch_shapes=[
                pltpu.VMEM((seqs, seq, feats), bf), pltpu.VMEM((3 * width, feats), bf), tables_t, lines_t,
                pltpu.VMEM((rows, width), bf), outs_t, square, pair, low_pair,
                pltpu.SemaphoreType.DMA((4 * seqs + 2 + heads,)),
            ],
            out_shape=[
                sds((seqs, 3 * width, seq), bf), sds((rows, width), bf), sds((seqs, width, seq), f32),
                sds((seqs, 8, seq), f32), sds((seqs, 8, seq), f32),
            ],
            compiler_params=params(LIMIT),
            cost_estimate=pl.CostEstimate(flops=COST, bytes_accessed=1 << 20, transcendentals=0),
            name="attend",
        )(tokens, wt, wl, pos, gw, sm, segq, segk, gate_bias, after(order[i : i + 1], *deps))

    def attend_back(i, sources, front, dctx, base, *deps):
        wt, wl, sm, pos = sources
        qkv_t, _, out_t, lse, gate = front
        own = i == 0
        out_shape = [sds((rows, feats), f32)]
        out_specs = [hbm]
        scratch = [
            pltpu.VMEM((3 * width + 16, feats), bf), tables_t, lines_t, outs_t, pltpu.VMEM((seqs, width, seq), bf),
            pltpu.VMEM((seqs, seq, feats), f32), square, pair, pair, low_pair, low_pair,
            pltpu.VMEM((seqs, 3 * width + 16, seq), bf), pltpu.SemaphoreType.DMA((5 * seqs + 2 + heads,)),
        ]
        if own:
            out_shape += [sds((3 * width, feats), f32), sds((8, feats), f32), sds((heads, seq, seq), f32)]
            out_specs += [hbm, full, hbm]
            scratch += [
                pltpu.VMEM((3 * width, feats), f32), pltpu.VMEM((seqs, seq, feats), bf), lines_t, tables_t,
                pltpu.SemaphoreType.DMA((heads + 1 + seqs,)),
            ]
        return pl.pallas_call(
            functools.partial(attend_back_kernel, heads, hd, i),
            in_specs=[hbm] * 8 + [full] * 4 + [smem] + [full] * 2,
            out_specs=out_specs,
            scratch_shapes=scratch,
            out_shape=out_shape,
            compiler_params=params(LIMIT),
            cost_estimate=pl.CostEstimate(flops=COST, bytes_accessed=1 << 20, transcendentals=0),
            name="attend_back",
        )(
            wt, wl, pos, qkv_t, out_t, dctx, base, tokens, gw, sm, segq, segk, after(order[i : i + 1], *deps), lse, gate
        )

    def piece(w, parts=1):
        per = w.shape[0] // n_dp // parts
        w = w.reshape(parts, n_dp, per, w.shape[1])
        return lax.dynamic_index_in_dim(w, dp, 1, False).reshape(parts * per, -1)

    alike = [[m * n_dp + d for m in range(n_mp) for d in range(n_dp) if d % 2 == c] for c in range(2)]
    yx = dp // 2
    per2 = units // n_dp
    piece2 = lax.dynamic_slice_in_dim(fc2_weight, core * (units // 2) + yx * per2, per2, 0)
    half2 = lax.all_gather(piece2, ("mp", "dp"), axis_index_groups=alike)

    small, cuts = lines_of(after(rel_table.T, piece2), fc1_bias[None], qv_bias, gate_scale[None])
    w0 = jnp.concatenate([qkv_weight.transpose(0, 2, 1).reshape(3 * width, feats), out_weight], axis=0)
    piece0 = jnp.concatenate([piece(w0, 2), cuts], axis=0)
    w0 = w0.reshape(2, 2 * width, feats)
    z0 = [rotate(piece0, r, n_mp) for r in range(1, n_mp)]
    buckets_t = buckets.T
    pos_own = bias_of(after(buckets_t, piece0), small[None], heads, size)
    z0, pos_own = lax.optimization_barrier((z0, pos_own))
    z0 = jnp.stack(z0)

    mid = 2 * width // n_dp
    got = z0[:, 2 * mid :].astype(f32)
    smalls = (got[:, 0:4] + got[:, 4:8]) + got[:, 8:12]
    w1_rows = fc1_weight.T
    mid1 = units // n_dp // 2
    piece1 = lax.dynamic_slice(w1_rows.reshape(2, 2, n_dp // 2, mid1, feats), (core, 0, yx, 0, 0), (1, 2, 1, mid1, feats))
    piece1 = after(piece1.reshape(2 * mid1, feats), z0)
    own_sources = (w0, w0[1:], small[None], pos_own)
    spreads = [z0[:, :mid], z0[:, mid : 2 * mid]]
    routes = [plane[::-1], plane]
    covers = [lambda *deps: bias_of(after(buckets_t, *deps), smalls, heads, size), lambda *deps: attend(0, own_sources, *deps)]
    done = []
    for step in range(len(plane)):
        gots = [swap(v, route[step], n_dp) for v, route in zip(spreads, routes)]
        if step == 0:
            z1 = [rotate(piece1, r, n_mp) for r in range(1, n_mp)]
        if step < len(covers):
            result = covers[step](*spreads)
            gots, result = lax.optimization_barrier((gots, result))
            done.append(result)
        spreads = [joined(v, g, route[step], dp, route[:step]) for v, g, route in zip(spreads, gots, routes)]
    for step in range(len(plane), len(covers)):
        done.append(covers[step]())
    pos_rest, front = done
    fronts = [front]
    spreads, z1 = lax.optimization_barrier((spreads, z1))
    gots = [swap(v, 1, n_dp) for v in spreads]
    top, low = (joined(v, g, 1, dp, plane).reshape(others, 2 * width, feats) for v, g in zip(spreads, gots))
    rest_sources = (top, low, smalls, pos_rest)

    z1 = jnp.stack(z1)
    spreads = [z1[:, :mid1], z1[:, mid1:]]
    for step in range(len(plane)):
        gots = [swap(v, route[step], n_dp) for v, route in zip(spreads, routes)]
        if step + 1 < n_mp:
            result = attend(step + 1, rest_sources, *spreads)
            gots, result = lax.optimization_barrier((gots, result))
            fronts.append(result)
        spreads = [joined(v, g, route[step], dp, route[:step]) for v, g, route in zip(spreads, gots, routes)]
    half = others * units // 2
    w1a = jnp.stack(spreads, axis=1).reshape(half, feats)
    w1b = swap(w1a, 1, n_dp)
    w2a = half2.reshape(n_mp, units // 2, feats)
    w2b = swap(w2a, 1, n_dp)
    for i in range(len(fronts), n_mp):
        fronts.append(attend(i, rest_sources, w1a, w2a))
    ctxs = [f[1] for f in fronts]
    b1o = smalls[:, 2]
    b1a = jnp.where(core == 1, b1o[:, units // 2 :], b1o[:, : units // 2])
    b1b = jnp.where(core == 1, b1o[:, : units // 2], b1o[:, units // 2 :])

    vec = jnp.concatenate([out_bias, ln1_gain, ln1_bias, fc2_bias, ln2_gain, ln2_bias]).reshape(6, feats)
    tile = 256

    def row(n):
        return pl.BlockSpec((tile, n), lambda i: (i, 0))

    outs = pl.pallas_call(
        layer_kernel,
        grid=(rows // tile,),
        in_specs=[row(width)] * n_mp
        + [row(feats), row(feats)]
        + [hbm] * 5
        + [full] * 3
        + [hbm] * 3
        + [full, smem],
        out_specs=[
            row(feats), row(feats), pl.BlockSpec((n_mp, 1, width, tile), lambda i: (0, i * tile // seq, 0, i % (seq // tile))),
            row(feats), row(feats), row(feats), row(units), row(units), pl.BlockSpec((8, feats), lambda i: (0, 0)),
        ],
        scratch_shapes=[
            pltpu.VMEM((n_mp * width, feats), bf), pltpu.VMEM((n_mp * units, feats), bf), pltpu.VMEM((n_mp * units, feats), bf),
            pltpu.VMEM((tile, n_mp * units), bf), pltpu.VMEM((tile, n_mp * units), f32), pltpu.VMEM((tile, n_mp * units), bf),
            pltpu.SemaphoreType.DMA((8 + 2 * others,)),
        ],
        out_shape=[
            sds((rows, feats), f32), sds((rows, feats), f32), sds((n_mp, seqs, width, seq), bf), sds((rows, feats), bf),
            sds((rows, feats), bf), sds((rows, feats), bf), sds((rows, units), bf), sds((rows, units), bf), sds((8, feats), f32),
        ],
        compiler_params=params(LIMIT),
        cost_estimate=pl.CostEstimate(flops=4 * COST, bytes_accessed=1 << 24, transcendentals=0),
        name="layer",
    )(*ctxs, tokens, grad_out, out_weight, low, w1_rows, w1a, w1b, small, b1a, b1b, fc2_weight, w2a, w2b, vec, order)
    normed, grad_first = outs[:2]
    dctx = outs[2]
    hid_low, mix_low, first_low, act_own, pre_own, sums = outs[3:]

    def outer(a, b):
        return lax.dot_general(a, b, (((0,), (0,)), ((), ())), preferred_element_type=f32)

    big = jnp.concatenate([outer(ctxs[0], first_low), outer(hid_low, pre_own), outer(act_own, mix_low)], axis=0).astype(bf)
    back, dw, tiny, acc = attend_back(0, own_sources, front, dctx, grad_first, big)
    big = lax.psum_scatter(big, "dp", scatter_dimension=0, tiled=True)

    shared = tiny[:3]
    turned = [rotate(shared, r, n_mp) for r in range(1, n_mp)]
    table = table_grad(after(buckets_t, shared), acc, size)
    table, turned, big = lax.optimization_barrier((table, turned, big))
    big = lax.all_gather(big, "dp", tiled=True)
    turned = [shared] + list(turned)
    while len(turned) > 1:
        turned = [a + b for a, b in zip(turned[: len(turned) // 2], turned[len(turned) // 2 :])]
    table = jnp.pad(table, ((0, 0), (0, feats - table.shape[1])))
    extra = jnp.concatenate([sums, turned[0], tiny[3:], table], axis=0)
    count = extra.shape[0] // 2

    def parted(flip):
        def pick(v):
            v = v.reshape(2, -1, feats)
            return jnp.where((core == 1) != flip, v[1], v[0])

        return jnp.concatenate([pick(dw), pick(extra)])

    total = parted(False) + swap(parted(True), 1, n_dp)
    cut = dw.shape[0] // 2
    i = 1
    for bit in plane:
        low_part = lax.reduce_precision(total[cut:], 8, 7)
        sent = jnp.concatenate([total[:cut], low_part, total[cut:] - low_part])
        sent = lax.reduce_precision(sent, 8, 7).astype(bf)
        got = swap(sent, bit, n_dp)
        if i < n_mp:
            back = attend_back(i, rest_sources, fronts[i], dctx, back, sent)[0]
            got, back = lax.optimization_barrier((got, back))
            if i == n_mp - 2:
                big, back = lax.optimization_barrier((big, back))
            i += 1
        both = sent.astype(f32) + got.astype(f32)
        total = jnp.concatenate([both[:cut], both[cut : cut + count] + both[cut + count :]])
    got = swap(total, 1, n_dp)
    while i < n_mp:
        back = attend_back(i, rest_sources, fronts[i], dctx, back, total)[0]
        i += 1
    input_grad, got, big = lax.optimization_barrier((back, got, big))
    first = jnp.where(core == 1, got, total)
    second = jnp.where(core == 1, total, got)
    dw = jnp.concatenate([first[:cut], second[:cut]]).reshape(3, width, feats).transpose(0, 2, 1)
    extra = jnp.concatenate([first[cut:], second[cut:]])

    sums = extra[:8]
    halves = extra[8:10].reshape(2, n_mp * heads, hd).sum(axis=1)
    grad_gate_weight = jnp.repeat(halves, gates // 2, axis=0).T
    grad_gate_bias = jnp.repeat(extra[10, :2], gates // 2)
    dqv_bias = jnp.stack([extra[12, :width], extra[12, 2 * width : 3 * width]])
    grad_gate_scale = extra[13, :heads]
    lows = 16
    grad_table = extra[16:, : heads * lows].reshape(-1, heads, lows).transpose(0, 2, 1).reshape(-1, heads)[:size]
    big = big.astype(f32)
    grad_ow = big[:width]
    grad_fc1 = big[width : width + feats]
    grad_fc2 = big[width + feats :]
    return (
        normed, input_grad, dw, dqv_bias, grad_table, grad_gate_weight, grad_gate_bias, grad_gate_scale, grad_ow, sums[5],
        sums[3], sums[4], grad_fc1, sums[6], grad_fc2, sums[2], sums[0], sums[1],
    )


def solution(mesh):
    in_specs = (
        P("dp", None), P("dp", None), P(), P(None, None, "mp"), P(None, "mp"), P(None, "mp"), P(), P(), P("mp"),
        P("mp", None), P(), P(), P(), P(None, "mp"), P("mp"), P("mp", None), P(), P(), P(), P("dp", None),
    )
    out_specs = (
        P("dp", None), P("dp", None), P(None, None, "mp"), P(None, "mp"), P(None, "mp"), P(), P(), P("mp"),
        P("mp", None), P(), P(), P(), P(None, "mp"), P("mp"), P("mp", None), P(), P(), P(),
    )
    fn = functools.partial(body, mesh.shape["dp"], mesh.shape["mp"])
    return jax.shard_map(fn, mesh=mesh, in_specs=in_specs, out_specs=out_specs, check_vma=False)
```

time: 454 us -> 304 us (0.67)
  waiting for transfers between devices: 193 us -> 15 us
  blocking collectives: 44.9 us -> 0 us
  starting transfers between devices: 0.2 us -> 39 us
  Pallas kernels: 158 us -> 183 us
  other arithmetic: 7.66 us -> 17.6 us
  local copies, waits for them, and re-layouts: 29.6 us -> 23.5 us
    all_gather x4 -> x2, waiting for transfers between devices: 168 us -> 0.25 us  [the longest x1 0.23 us: body(): big = lax.all_gather(big, 'dp', tiled=True)]
    ppermute x0 -> x25, starting transfers between devices: none -> 38.7 us  [the longest x9 26 us: rotate(): return lax.ppermute(x, 'mp', [(i, (i + by) % n) for i in range(n)])]
    psum x1 -> x0, waiting for transfers between devices: 25.3 us -> none  [body(): big = lax.psum(big, 'dp').astype(f32)]
    pallas_call x5 -> x13, Pallas kernels: 158 us -> 183 us  [the longest x4 64.3 us: attend_back(): pl.pallas_call(functools.partial(attend_back_kernel, heads, hd, i), in_sp...]
    psum x1 -> x0, blocking collectives: 23.7 us -> none  [body(): little = lax.psum(little, 'dp')]
    unnamed x1 -> x0, blocking collectives: 21.1 us -> none
    reduce_scatter x0 -> x1, waiting for transfers between devices: none -> 7.58 us  [body(): big = lax.psum_scatter(big, 'dp', scatter_dimension=0, tiled=True)]
    ppermute x0 -> x25, waiting for transfers between devices: none -> 7.15 us  [the longest x16 6.61 us: swap(): return lax.ppermute(x, axis, [(i, i ^ bit) for i in range(n)])]
  transfers between devices with their start and end apart: 5 -> 28, of which waited for: 5 -> 8; matrix products, arithmetic and copies ran while one was open for 5% -> 8% of each run, Pallas kernels for 14% -> 46%
where the time goes in v2:
time: 304 us; the launch traced here: 299 us
  Pallas kernels  183 us (60%)
  starting transfers between devices  39 us (13%)
  local copies, waits for them, and re-layouts  23.5 us (8%)
  other arithmetic  17.6 us (6%)
  waiting for transfers between devices  15 us (5%)
  between operations  14.9 us (5%)
  matrix products  6.5 us (2%)
    pallas_call x4, Pallas kernels, attend_back(): pl.pallas_call(functools.partial(attend_back_kernel, heads, hd, i), in_sp...  64.3 us
    pallas_call x1, Pallas kernels, body(): pl.pallas_call(layer_kernel, grid=(rows // tile,), in_specs=[row(width)]...  43.7 us
    pallas_call x4, Pallas kernels, attend(): pl.pallas_call(functools.partial(attend_kernel, heads, hd, max(i - 1, 0))...  42.9 us
    ppermute x9, starting transfers between devices, rotate(): return lax.ppermute(x, 'mp', [(i, (i + by) % n) for i in range(n)])  26 us
    pallas_call x2, Pallas kernels, bias_of(): pl.pallas_call(functools.partial(bias_kernel, heads * groups, -(-size //...  18.3 us
    ppermute x16, starting transfers between devices, swap(): return lax.ppermute(x, axis, [(i, i ^ bit) for i in range(n)])  12.7 us
    pallas_call x1, Pallas kernels, table_grad(): pl.pallas_call(functools.partial(table_kernel, heads, tops, lows), out_sh...  11.7 us
    reduce_scatter x1, waiting for transfers between devices, body(): big = lax.psum_scatter(big, 'dp', scatter_dimension=0, tiled=True)  7.58 us
  transfers between devices with their start and end apart: 28, of which 8 were waited for; matrix products, arithmetic and copies ran while one was open for 8% of the time, Pallas kernels for 46%

profile of v2, /device:TPU:0, one launch (start us, length us, event | category | flops | bytes accessed | tf_op | source)
XLA Modules:
  0.0 299.1 jit_solution(16063569936263953755)
XLA Ops:
  7.3 1.7 constant_dynamic-slice_fusion.1
  8.9 1.3 broadcast_in_dim.22.b1_ref
  10.2 1.3 pad_maximum_fusion.5
  11.6 1.7 lines.1
  13.3 1.4 pad_maximum_fusion.16
  14.7 3.0 %collective-permute-start = (bf16[112,768]{1,0:T(8,128)(2,1)}, bf16[112,768]{1,0:T(8,128)(2,1)}, u32[]{:S(2)}, u32[]{:S(2)}) collective-permute-start(bf16[112,768]{1,0:T(8,128)(2,1)} %pad_maximum_fusion.16), channel_id=1, source_target_pairs={{0,1},{1,2},{2,3},{3,0},{4,5},{5,6},{6,7},{7,4},{8,9},{9,10},{10,1... | collective-permute-start | bytes 516104 | tf_op jit(solution)/shard_map/ppermute | solution.py:552
  17.7 2.6 collective-permute-start.1
  20.3 1.3 collective-permute-start.2
  21.7 1.3 copy.46
  23.7 7.6 %pos_bias.2.pos_hbm = f32[3,512,512]{2,1,0:T(8,128)} custom-call(s32[512,512]{1,0:T(8,128)} %bitcast.128, f32[1,4,768]{2,1,0:T(4,128)} %bitcast.138), custom_call_target="tpu_custom_call" | custom-call | flops 3000000000 | bytes 1048576 | tf_op jit(solution)/shard_map/pos_bias/pallas_call | solution.py:90
  31.9 1.1 pad_maximum_fusion.10
  33.1 1.6 collective-permute-start.3
  34.7 1.5 collective-permute-start.4
  36.8 10.7 %pos_bias.3.pos_hbm = f32[9,512,512]{2,1,0:T(8,128)} custom-call(s32[512,512]{1,0:T(8,128)} %bitcast.129, f32[3,4,768]{2,1,0:T(4,128)} %slice_add_fusion.2.small_ref), custom_call_target="tpu_custom_call" | custom-call | flops 3000000000 | bytes 1048576 | tf_op jit(solution)/shard_map/pos_bias/pallas_call | solution.py:90
  51.8 1.4 tile.10.gw_ref
  54.1 5.8 %collective-permute-start.7 = (bf16[96,768]{1,0:T(8,128)(2,1)S(1)}, bf16[96,768]{1,0:T(8,128)(2,1)}, u32[]{:S(2)}, u32[]{:S(2)}) collective-permute-start(bf16[96,768]{1,0:T(8,128)(2,1)S(1)} %bitcast.132), channel_id=1, source_target_pairs={{0,1},{1,2},{2,3},{3,0},{4,5},{5,6},{6,7},{7,4},{8,9},{9,10},{10,1... | collective-permute-start | bytes 442376 | tf_op jit(solution)/shard_map/ppermute | solution.py:552
  59.9 1.5 collective-permute-start.8
  62.4 10.7 %attend.4 = (bf16[2,576,512]{2,1,0:T(8,128)(2,1)}, bf16[1024,192]{1,0:T(8,128)(2,1)}, f32[2,192,512]{2,1,0:T(8,128)}, f32[2,8,512]{2,1,0:T(8,128)}, f32[2,8,512]{2,1,0:T(8,128)}) custom-call(bf16[1024,768]{1,0:T(8,128)(2,1)} %x_hbm.15, bf16[2,384,768]{2,1,0:T(8,128)(2,1)} %bitcast.119, bf16[1,384,768]{2,1,0:T(8,128)(2,1)} %fusion.3.wl_hbm, ...), custom_call_target="tpu_custom_call" | custom-call | flops 3000000000 | bytes 1048576 | tf_op jit(solution)/shard_map/attend/pallas_call | solution.py:604
  73.3 1.1 select_bitcast_fusion.11
  75.1 1.1 pad_maximum_fusion.13
  77.0 1.8 collective-permute-start.10
  78.8 1.6 collective-permute-start.11
  80.7 1.4 copy.52
  82.4 1.4 copy.51
  83.8 10.8 %attend.5 = (bf16[2,576,512]{2,1,0:T(8,128)(2,1)}, bf16[1024,192]{1,0:T(8,128)(2,1)}, f32[2,192,512]{2,1,0:T(8,128)}, f32[2,8,512]{2,1,0:T(8,128)}, f32[2,8,512]{2,1,0:T(8,128)}) custom-call(bf16[1024,768]{1,0:T(8,128)(2,1)} %x_hbm.15, bf16[3,384,768]{2,1,0:T(8,128)(2,1)} %bitcast.112, bf16[3,384,768]{2,1,0:T(8,128)(2,1)} %bitcast.105, ...), custom_call_target="tpu_custom_call" | custom-call | flops 3000000000 | bytes 1048576 | tf_op jit(solution)/shard_map/attend/pallas_call | solution.py:604
  94.7 1.1 select_bitcast_fusion.13
  96.7 10.7 %attend.6 = (bf16[2,576,512]{2,1,0:T(8,128)(2,1)}, bf16[1024,192]{1,0:T(8,128)(2,1)}, f32[2,192,512]{2,1,0:T(8,128)}, f32[2,8,512]{2,1,0:T(8,128)}, f32[2,8,512]{2,1,0:T(8,128)}) custom-call(bf16[1024,768]{1,0:T(8,128)(2,1)} %x_hbm.15, bf16[3,384,768]{2,1,0:T(8,128)(2,1)} %bitcast.113, bf16[3,384,768]{2,1,0:T(8,128)(2,1)} %bitcast.106, ...), custom_call_target="tpu_custom_call" | custom-call | flops 3000000000 | bytes 1048576 | tf_op jit(solution)/shard_map/attend/pallas_call | solution.py:604
  111.2 10.6 %attend.7 = (bf16[2,576,512]{2,1,0:T(8,128)(2,1)}, bf16[1024,192]{1,0:T(8,128)(2,1)}, f32[2,192,512]{2,1,0:T(8,128)}, f32[2,8,512]{2,1,0:T(8,128)}, f32[2,8,512]{2,1,0:T(8,128)}) custom-call(bf16[1024,768]{1,0:T(8,128)(2,1)} %x_hbm.15, bf16[3,384,768]{2,1,0:T(8,128)(2,1)} %bitcast.114, bf16[3,384,768]{2,1,0:T(8,128)(2,1)} %bitcast.107, ...), custom_call_target="tpu_custom_call" | custom-call | flops 3000000000 | bytes 1048576 | tf_op jit(solution)/shard_map/attend/pallas_call | solution.py:604
  121.9 43.7 %layer.1 = (f32[1024,768]{1,0:T(8,128)}, f32[1024,768]{1,0:T(8,128)}, bf16[4,2,192,512]{3,2,1,0:T(8,128)(2,1)}, bf16[1024,768]{1,0:T(8,128)(2,1)}, bf16[1024,768...) custom-call(bf16[1024,192]{1,0:T(8,128)(2,1)} %get-tuple-element.130, ...), custom_call_target="tpu_custom_call" | custom-call | flops 12000000000 | bytes 16777216 | tf_op jit(solution)/shard_map/layer/pallas_call | solution.py:731
  165.7 2.0 convolution_convert_fusion.2
  167.7 3.0 %convolution_convert_fusion.1 = bf16[768,768]{1,0:T(8,128)(2,1)S(1)} fusion(bf16[1024,768]{1,0:T(8,128)(2,1)S(1)} %copy-done.22, bf16[1024,768]{1,0:T(8,128)(2,1)} %get-tuple-element.169), kind=kOutput, calls=%fused_computation.6 | convolution fusion | flops 1208549376 | bytes 4325376 | tf_op jit(solution)/shard_map/dot_general | solution.py:762
  170.8 1.5 convolution_convert_fusion
  172.3 1.6 pad_maximum_fusion
  174.2 18.9 %attend_back.4 = (f32[1024,768]{1,0:T(8,128)}, f32[576,768]{1,0:T(8,128)}, f32[8,768]{1,0:T(8,128)}, f32[3,512,512]{2,1,0:T(8,128)}) custom-call(bf16[2,384,768]{2,1,0:T(8,128)(2,1)} %bitcast.120, bf16[1,384,768]{2,1,0:T(8,128)(2,1)} %fusion.3.wl_hbm, f32[3,512,512]{2,1,0:T(8,128)} %pos_bias.2.pos_hbm, bf16[2,576,512]{2,1,0:T(8,128)(2,1)} %get-tuple-element.164.qkv_hbm, ...), custom_call_target="tpu_custom_call" | custom-call | flops 3000000000 | bytes 1048576 | tf_op jit(solution)/shard_map/attend_back/pallas_call | solution.py:640
  193.8 8.3 %collective-permute-start.18 = (f32[3,768]{1,0:T(4,128)S(1)}, f32[3,768]{1,0:T(4,128)S(1)}, u32[]{:S(2)}, u32[]{:S(2)}) collective-permute-start(f32[3,768]{1,0:T(4,128)S(1)} %slice.206), channel_id=1, source_target_pairs={{0,1},{1,2},{2,3},{3,0},{4,5},{5,6},{6,7},{7,4},{8,9},{9,10},{10,1... | collective-permute-start | bytes 27656 | tf_op jit(solution)/shard_map/ppermute | solution.py:552
  202.1 1.8 collective-permute-start.19
  204.4 1.6 slice_select_fusion.1
  206.0 11.7 %table_grad.1 = f32[24,48]{1,0:T(8,128)} custom-call(s32[512,512]{1,0:T(8,128)} %bitcast.130, f32[3,512,512]{2,1,0:T(8,128)} %get-tuple-element.177.val_ref), custom_call_target="tpu_custom_call" | custom-call | flops 3000000000 | bytes 1048576 | tf_op jit(solution)/shard_map/table_grad/pallas_call | solution.py:542
  217.8 7.6 %reduce-scatter.2.cloned.1.call-done = bf16[216,768]{1,0:T(8,128)(2,1)} async-done(((bf16[1728,768]{1,0:T(8,128)(2,1)}), bf16[216,768]{1,0:T(8,128)(2,1)}) %reduce-scatter.2.cloned.1.call-update) | async-done | bytes 331792 | tf_op jit(solution)/shard_map/reduce_scatter | solution.py:766
  227.1 2.5 collective-permute-done.21
  229.9 1.5 collective-permute-start.22
  231.3 15.0 %attend_back.5.base_hbm = f32[1024,768]{1,0:T(8,128)} custom-call(bf16[3,384,768]{2,1,0:T(8,128)(2,1)} %bitcast.115, bf16[3,384,768]{2,1,0:T(8,128)(2,1)} %bitcast.109, f32[9,512,512]{2,1,0:T(8,128)} %pos_bias.3.pos_hbm, bf16[2,576,512]{2,1,0:T(8,128)(2,1)} %get-tuple-element.185.qkv_hbm, f32[2,192,512]{2,1,0:T(8,128)} %get-tuple-element.186.out_hbm, ...), custom_call_target="tpu_custom_call" | custom-call | flops 3000000000 | bytes 1048576 | tf_op jit(solution)/shard_map/attend_back/pallas_call | solution.py:640
  247.3 1.5 collective-permute-start.23
  248.8 15.4 %attend_back.6.base_hbm = f32[1024,768]{1,0:T(8,128)} custom-call(bf16[3,384,768]{2,1,0:T(8,128)(2,1)} %bitcast.116, bf16[3,384,768]{2,1,0:T(8,128)(2,1)} %bitcast.110, f32[9,512,512]{2,1,0:T(8,128)} %pos_bias.3.pos_hbm, bf16[2,576,512]{2,1,0:T(8,128)(2,1)} %get-tuple-element.192.qkv_hbm, f32[2,192,512]{2,1,0:T(8,128)} %get-tuple-element.193.out_hbm, ...), custom_call_target="tpu_custom_call" | custom-call | flops 3000000000 | bytes 1048576 | tf_op jit(solution)/shard_map/attend_back/pallas_call | solution.py:640
  264.1 3.0 %collective-permute-done.23 = bf16[328,768]{1,0:T(8,128)(2,1)S(1)} collective-permute-done((bf16[328,768]{1,0:T(8,128)(2,1)S(1)}, bf16[328,768]{1,0:T(8,128)(2,1)S(1)}, u32[]{:S(2)}, u32[]{:S(2)}) %collective-permute-start.23) | collective-permute-done | bytes 503840 | tf_op jit(solution)/shard_map/ppermute | solution.py:556
  267.7 15.1 %attend_back.7 = f32[1024,768]{1,0:T(8,128)} custom-call(bf16[3,384,768]{2,1,0:T(8,128)(2,1)} %bitcast.117, bf16[3,384,768]{2,1,0:T(8,128)(2,1)} %bitcast.111, f32[9,512,512]{2,1,0:T(8,128)} %pos_bias.3.pos_hbm, bf16[2,576,512]{2,1,0:T(8,128)(2,1)} %get-tuple-element.161.qkv_hbm, f32[2,192,512]{2,1,0:T(8,128)} %get-tuple-element.162.out_hbm, ...), custom_call_target="tpu_custom_call" | custom-call | flops 3000000000 | bytes 1048576 | tf_op jit(solution)/shard_map/attend_back/pallas_call | solution.py:640
  284.8 2.5 fusion.6
  290.4 1.3 pad_maximum_fusion.4
  (169 shorter events, 25.4 us)
Async XLA Ops:
  7.2 100.6 %all-gather.6.cloned.1.call-start = ((), (), s32[]{:S(2)}) async-start(), calls=%async_computation.3 | async-start | bytes 2506752 | tf_op jit(solution)/shard_map/all_gather | solution.py:662
  7.2 14.5 %copy-start.7 = (s32[512,512]{1,0:T(8,128)S(1)}, s32[512,512]{1,0:T(8,128)}, u32[]{:S(2)}) copy-start(s32[512,512]{1,0:T(8,128)} %param.22) | copy-start | bytes 3145732
  11.5 12.2 %copy-start.1 = (bf16[768,768]{1,0:T(8,128)(2,1)}, bf16[768,768]{1,0:T(8,128)(2,1)S(1)}, u32[]{:S(2)}) copy-start(bf16[768,768]{1,0:T(8,128)(2,1)S(1)} %pad_maximum_fusion.5) | copy-start | bytes 3538948
  11.6 11.5 %copy-start.6 = (bf16[768,768]{1,0:T(8,128)(2,1)S(1)}, bf16[768,768]{1,0:T(8,128)(2,1)}, u32[]{:S(2)}) copy-start(bf16[768,768]{1,0:T(8,128)(2,1)} %param.33) | copy-start | bytes 3538948
  14.7 16.7 %collective-permute-start = (bf16[112,768]{1,0:T(8,128)(2,1)}, bf16[112,768]{1,0:T(8,128)(2,1)}, u32[]{:S(2)}, u32[]{:S(2)}) collective-permute-start(bf16[112,768]{1,0:T(8,128)(2,1)} %pad_maximum_fusion.16), channel_id=1, source_target_pairs={{0,1},{1,2},{2,3},{3,0},{4,5},{5,6},{6,7},{7,4},{8,9},{9,10},{10,1... | collective-permute-start | bytes 516104 | tf_op jit(solution)/shard_map/ppermute | solution.py:552
  17.7 14.2 %collective-permute-start.1 = (bf16[112,768]{1,0:T(8,128)(2,1)}, bf16[112,768]{1,0:T(8,128)(2,1)}, u32[]{:S(2)}, u32[]{:S(2)}) collective-permute-start(bf16[112,768]{1,0:T(8,128)(2,1)} %pad_maximum_fusion.16), channel_id=1, source_target_pairs={{0,2},{1,3},{2,0},{3,1},{4,6},{5,7},{6,4},{7,5},{8,10},{9,11},{10,... | collective-permute-start | bytes 516104 | tf_op jit(solution)/shard_map/ppermute | solution.py:552
  20.3 11.6 %collective-permute-start.2 = (bf16[112,768]{1,0:T(8,128)(2,1)}, bf16[112,768]{1,0:T(8,128)(2,1)}, u32[]{:S(2)}, u32[]{:S(2)}) collective-permute-start(bf16[112,768]{1,0:T(8,128)(2,1)} %pad_maximum_fusion.16), channel_id=1, source_target_pairs={{0,3},{1,0},{2,1},{3,2},{4,7},{5,4},{6,5},{7,6},{8,11},{9,8},{10,9... | collective-permute-start | bytes 516104 | tf_op jit(solution)/shard_map/ppermute | solution.py:552
  21.7 203.7 %reduce-scatter.2.cloned.1.call-start = ((), (), s32[]{:S(2)}) async-start(), calls=%async_computation.1 | async-start | bytes 2985984 | tf_op jit(solution)/shard_map/reduce_scatter | solution.py:766
  23.7 7.6 %copy-start.4 = (bf16[768,768]{0,1:T(8,128)(2,1)}, bf16[768,768]{0,1:T(8,128)(2,1)S(1)}, u32[]{:S(2)}) copy-start(bf16[768,768]{0,1:T(8,128)(2,1)S(1)} %copy.49) | copy-start | bytes 3538948
  31.3 17.6 %copy-start.11 = (s32[4]{0:T(128)}, s32[4]{0:T(128)S(1)}, u32[]{:S(2)}) copy-start(s32[4]{0:T(128)S(1)} %and_select_fusion.at_ref) | copy-start | bytes 52
  33.1 14.4 %collective-permute-start.3 = (bf16[3,48,768]{2,1,0:T(8,128)(2,1)S(1)}, bf16[3,48,768]{2,1,0:T(8,128)(2,1)S(1)}, u32[]{:S(2)}, u32[]{:S(2)}) collective-permute-start(bf16[3,48,768]{2,1,0:T(8,128)(2,1)S(1)} %get-tuple-element.250), channel_id=1, source_target_pairs={{0,16},{4,20},{8,24},{12,28},{16,0},{20,4},{24,8},{28,12},{1,17},{... | collective-permute-start | bytes 663560 | tf_op jit(solution)/shard_map/ppermute | solution.py:556
  34.7 12.9 %collective-permute-start.4 = (bf16[3,48,768]{2,1,0:T(8,128)(2,1)S(1)}, bf16[3,48,768]{2,1,0:T(8,128)(2,1)S(1)}, u32[]{:S(2)}, u32[]{:S(2)}) collective-permute-start(bf16[3,48,768]{2,1,0:T(8,128)(2,1)S(1)} %get-tuple-element.249), channel_id=1, source_target_pairs={{0,8},{4,12},{8,0},{12,4},{16,24},{20,28},{24,16},{28,20},{1,9},{5... | collective-permute-start | bytes 663560 | tf_op jit(solution)/shard_map/ppermute | solution.py:556
  47.5 2.0 copy-start.10
  47.5 3.6 %copy-start.18 = (bf16[64,8]{0,1:T(8,128)(2,1)S(1)}, bf16[64,8]{0,1:T(8,128)(2,1)}, u32[]{:S(2)}) copy-start(bf16[64,8]{0,1:T(8,128)(2,1)} %param.26) | copy-start | bytes 3076
  47.5 5.7 %copy-start.2 = (bf16[3,768,192]{1,2,0:T(8,128)(2,1)S(1)}, bf16[3,768,192]{1,2,0:T(8,128)(2,1)}, u32[]{:S(2)}) copy-start(bf16[3,768,192]{1,2,0:T(8,128)(2,1)} %param.23) | copy-start | bytes 2654212
  47.5 5.7 %copy-start.5 = (bf16[192,768]{1,0:T(8,128)(2,1)S(1)}, bf16[192,768]{1,0:T(8,128)(2,1)}, u32[]{:S(2)}) copy-start(bf16[192,768]{1,0:T(8,128)(2,1)} %ow0_hbm.1) | copy-start | bytes 884740
  47.7 25.5 %collective-permute-start.6 = (bf16[3,2,48,768]{3,2,0,1:T(8,128)(2,1)S(1)}, bf16[3,2,48,768]{3,2,0,1:T(8,128)(2,1)S(1)}, u32[]{:S(2)}, u32[]{:S(2)}) collective-permute-start(bf16[3,2,48,768]{3,2,0,1:T(8,128)(2,1)S(1)} %pad_maximum_fusion.12), channel_id=1, source_target_pairs={{0,16},{4,20},{8,24},{12,28},{16,0},{20,4},{24,8},{28,12},{1,17},{... | collective-permute-start | bytes 1327112 | tf_op jit(solution)/shard_map/ppermute | solution.py:556
  48.3 24.9 %collective-permute-start.5 = (bf16[3,2,48,768]{3,2,0,1:T(8,128)(2,1)S(1)}, bf16[3,2,48,768]{3,2,0,1:T(8,128)(2,1)}, u32[]{:S(2)}, u32[]{:S(2)}) collective-permute-start(bf16[3,2,48,768]{3,2,0,1:T(8,128)(2,1)S(1)} %pad_maximum_fusion.11), channel_id=1, source_target_pairs={{0,8},{4,12},{8,0},{12,4},{16,24},{20,28},{24,16},{28,20},{1,9},{5... | collective-permute-start | bytes 1327112 | tf_op jit(solution)/shard_map/ppermute | solution.py:556
  54.1 20.4 %collective-permute-start.7 = (bf16[96,768]{1,0:T(8,128)(2,1)S(1)}, bf16[96,768]{1,0:T(8,128)(2,1)}, u32[]{:S(2)}, u32[]{:S(2)}) collective-permute-start(bf16[96,768]{1,0:T(8,128)(2,1)S(1)} %bitcast.132), channel_id=1, source_target_pairs={{0,1},{1,2},{2,3},{3,0},{4,5},{5,6},{6,7},{7,4},{8,9},{9,10},{10,1... | collective-permute-start | bytes 442376 | tf_op jit(solution)/shard_map/ppermute | solution.py:552
  59.9 14.6 %collective-permute-start.8 = (bf16[96,768]{1,0:T(8,128)(2,1)S(1)}, bf16[96,768]{1,0:T(8,128)(2,1)}, u32[]{:S(2)}, u32[]{:S(2)}) collective-permute-start(bf16[96,768]{1,0:T(8,128)(2,1)S(1)} %bitcast.133), channel_id=1, source_target_pairs={{0,2},{1,3},{2,0},{3,1},{4,6},{5,7},{6,4},{7,5},{8,10},{9,11},{10,... | collective-permute-start | bytes 442376 | tf_op jit(solution)/shard_map/ppermute | solution.py:552
  61.5 13.1 %collective-permute-start.9 = (bf16[96,768]{1,0:T(8,128)(2,1)S(1)}, bf16[96,768]{1,0:T(8,128)(2,1)}, u32[]{:S(2)}, u32[]{:S(2)}) collective-permute-start(bf16[96,768]{1,0:T(8,128)(2,1)S(1)} %bitcast.134), channel_id=1, source_target_pairs={{0,3},{1,0},{2,1},{3,2},{4,7},{5,4},{6,5},{7,6},{8,11},{9,8},{10,9... | collective-permute-start | bytes 442376 | tf_op jit(solution)/shard_map/ppermute | solution.py:552
  74.6 5.9 %collective-permute-start.13 = (bf16[3,2,2,48,768]{4,3,0,2,1:T(8,128)(2,1)S(1)}, bf16[3,2,2,48,768]{4,3,0,2,1:T(8,128)(2,1)S(1)}, u32[]{:S(2)}, u32[]{:S(2)}) collective-permute-start(bf16[3,2,2,48,768]{4,3,0,2,1:T(8,128)(2,1)S(1)} %get-tuple-element.138), channel_id=1, source_target_pairs={{0,4},{4,0},{8,12},{12,8},{16,20},{20,16},{24,28},{28,24},{1,5},{5... | collective-permute-start | bytes 2654216 | tf_op jit(solution)/shard_map/ppermute | solution.py:556
  74.6 7.5 %collective-permute-start.12 = (bf16[3,2,2,48,768]{4,3,0,2,1:T(8,128)(2,1)S(1)}, bf16[3,2,2,48,768]{4,3,0,2,1:T(8,128)(2,1)S(1)}, u32[]{:S(2)}, u32[]{:S(2)}) collective-permute-start(bf16[3,2,2,48,768]{4,3,0,2,1:T(8,128)(2,1)S(1)} %get-tuple-element.137), channel_id=1, source_target_pairs={{0,4},{4,0},{8,12},{12,8},{16,20},{20,16},{24,28},{28,24},{1,5},{5... | collective-permute-start | bytes 2654216 | tf_op jit(solution)/shard_map/ppermute | solution.py:556
  77.0 17.6 %collective-permute-start.10 = (bf16[3,48,768]{2,1,0:T(8,128)(2,1)}, bf16[3,48,768]{2,1,0:T(8,128)(2,1)}, u32[]{:S(2)}, u32[]{:S(2)}) collective-permute-start(bf16[3,48,768]{2,1,0:T(8,128)(2,1)} %get-tuple-element.254), channel_id=1, source_target_pairs={{0,16},{4,20},{8,24},{12,28},{16,0},{20,4},{24,8},{28,12},{1,17},{... | collective-permute-start | bytes 663560 | tf_op jit(solution)/shard_map/ppermute | solution.py:556
  78.8 15.9 %collective-permute-start.11 = (bf16[3,48,768]{2,1,0:T(8,128)(2,1)}, bf16[3,48,768]{2,1,0:T(8,128)(2,1)}, u32[]{:S(2)}, u32[]{:S(2)}) collective-permute-start(bf16[3,48,768]{2,1,0:T(8,128)(2,1)} %get-tuple-element.253), channel_id=1, source_target_pairs={{0,8},{4,12},{8,0},{12,4},{16,24},{20,28},{24,16},{28,20},{1,9},{5... | collective-permute-start | bytes 663560 | tf_op jit(solution)/shard_map/ppermute | solution.py:556
  95.8 11.7 %collective-permute-start.15 = (bf16[3,2,48,768]{3,2,0,1:T(8,128)(2,1)S(1)}, bf16[3,2,48,768]{3,2,0,1:T(8,128)(2,1)S(1)}, u32[]{:S(2)}, u32[]{:S(2)}) collective-permute-start(bf16[3,2,48,768]{3,2,0,1:T(8,128)(2,1)S(1)} %pad_maximum_fusion.15), channel_id=1, source_target_pairs={{0,16},{4,20},{8,24},{12,28},{16,0},{20,4},{24,8},{28,12},{1,17},{... | collective-permute-start | bytes 1327112 | tf_op jit(solution)/shard_map/ppermute | solution.py:556
  96.3 11.4 %collective-permute-start.14 = (bf16[3,2,48,768]{3,2,0,1:T(8,128)(2,1)S(1)}, bf16[3,2,48,768]{3,2,0,1:T(8,128)(2,1)S(1)}, u32[]{:S(2)}, u32[]{:S(2)}) collective-permute-start(bf16[3,2,48,768]{3,2,0,1:T(8,128)(2,1)S(1)} %pad_maximum_fusion.14), channel_id=1, source_target_pairs={{0,8},{4,12},{8,0},{12,4},{16,24},{20,28},{24,16},{28,20},{1,9},{5... | collective-permute-start | bytes 1327112 | tf_op jit(solution)/shard_map/ppermute | solution.py:556
  107.8 14.2 %collective-permute-start.17 = (bf16[4,384,768]{2,1,0:T(8,128)(2,1)}, bf16[4,384,768]{2,1,0:T(8,128)(2,1)}, u32[]{:S(2)}, u32[]{:S(2)}) collective-permute-start(bf16[4,384,768]{2,1,0:T(8,128)(2,1)} %bitcast.145), channel_id=1, source_target_pairs={{0,4},{4,0},{8,12},{12,8},{16,20},{20,16},{24,28},{28,24},{1,5},{5... | collective-permute-start | bytes 7077896 | tf_op jit(solution)/shard_map/ppermute | solution.py:556
  108.3 0.8 copy-start.15
  108.3 0.9 copy-start.16
  108.4 0.9 copy-start.17
  108.6 13.3 %copy-start.3 = (bf16[3,2,2,2,48,768]{5,4,3,2,1,0:T(8,128)(2,1)}, bf16[3,2,2,2,48,768]{5,4,3,2,1,0:T(8,128)(2,1)S(1)}, u32[]{:S(2)}) copy-start(bf16[3,2,2,2,48,768]{5,4,3,2,1,0:T(8,128)(2,1)S(1)} %copy.56) | copy-start | bytes 5308420
  108.6 13.3 %collective-permute-start.16 = (bf16[1152,768]{1,0:T(8,128)(2,1)S(1)}, bf16[1152,768]{1,0:T(8,128)(2,1)}, u32[]{:S(2)}, u32[]{:S(2)}) collective-permute-start(bf16[1152,768]{1,0:T(8,128)(2,1)S(1)} %bitcast.123), channel_id=1, source_target_pairs={{0,4},{4,0},{8,12},{12,8},{16,20},{20,16},{24,28},{28,24},{1,5},{5... | collective-permute-start | bytes 5308424 | tf_op jit(solution)/shard_map/ppermute | solution.py:556
  121.9 43.8 %copy-start.19 = (bf16[1024,192]{1,0:T(8,128)(2,1)S(1)}, bf16[1024,192]{1,0:T(8,128)(2,1)}, u32[]{:S(2)}) copy-start(bf16[1024,192]{1,0:T(8,128)(2,1)} %get-tuple-element.130.ctx0_ref) | copy-start | bytes 1179652
  165.7 2.1 copy-start.22
  167.7 3.0 %copy-start.20 = (bf16[1024,768]{1,0:T(8,128)(2,1)S(1)}, bf16[1024,768]{1,0:T(8,128)(2,1)}, u32[]{:S(2)}) copy-start(bf16[1024,768]{1,0:T(8,128)(2,1)} %get-tuple-element.171) | copy-start | bytes 4718596
  167.7 3.0 %copy-start.21 = (bf16[1024,768]{1,0:T(8,128)(2,1)S(1)}, bf16[1024,768]{1,0:T(8,128)(2,1)}, u32[]{:S(2)}) copy-start(bf16[1024,768]{1,0:T(8,128)(2,1)} %get-tuple-element.170) | copy-start | bytes 4718596
  173.9 93.8 %all-gather.4.cloned.1.call-start = ((), (), s32[]{:S(2)}) async-start(), calls=%async_computation.2 | async-start | bytes 2985984 | tf_op jit(solution)/shard_map/all_gather | solution.py:772
  193.8 23.9 %collective-permute-start.18 = (f32[3,768]{1,0:T(4,128)S(1)}, f32[3,768]{1,0:T(4,128)S(1)}, u32[]{:S(2)}, u32[]{:S(2)}) collective-permute-start(f32[3,768]{1,0:T(4,128)S(1)} %slice.206), channel_id=1, source_target_pairs={{0,1},{1,2},{2,3},{3,0},{4,5},{5,6},{6,7},{7,4},{8,9},{9,10},{10,1... | collective-permute-start | bytes 27656 | tf_op jit(solution)/shard_map/ppermute | solution.py:552
  202.1 15.7 %collective-permute-start.19 = (f32[3,768]{1,0:T(4,128)S(1)}, f32[3,768]{1,0:T(4,128)S(1)}, u32[]{:S(2)}, u32[]{:S(2)}) collective-permute-start(f32[3,768]{1,0:T(4,128)S(1)} %slice.206), channel_id=1, source_target_pairs={{0,2},{1,3},{2,0},{3,1},{4,6},{5,7},{6,4},{7,5},{8,10},{9,11},{10,... | collective-permute-start | bytes 27656 | tf_op jit(solution)/shard_map/ppermute | solution.py:552
  203.9 13.8 %collective-permute-start.20 = (f32[3,768]{1,0:T(4,128)S(1)}, f32[3,768]{1,0:T(4,128)S(1)}, u32[]{:S(2)}, u32[]{:S(2)}) collective-permute-start(f32[3,768]{1,0:T(4,128)S(1)} %slice.206), channel_id=1, source_target_pairs={{0,3},{1,0},{2,1},{3,2},{4,7},{5,4},{6,5},{7,6},{8,11},{9,8},{10,9... | collective-permute-start | bytes 27656 | tf_op jit(solution)/shard_map/ppermute | solution.py:552
  206.0 11.7 %copy-start.8 = (f32[8,768]{1,0:T(8,128)S(1)}, f32[8,768]{1,0:T(8,128)}, u32[]{:S(2)}) copy-start(f32[8,768]{1,0:T(8,128)} %get-tuple-element.175) | copy-start | bytes 73732
  206.0 20.1 %copy-start.9 = (f32[8,768]{1,0:T(8,128)S(1)}, f32[8,768]{1,0:T(8,128)}, u32[]{:S(2)}) copy-start(f32[8,768]{1,0:T(8,128)} %get-tuple-element.181) | copy-start | bytes 73732
  227.0 2.6 collective-permute-start.21
  229.9 17.1 %collective-permute-start.22 = (bf16[328,768]{1,0:T(8,128)(2,1)S(1)}, bf16[328,768]{1,0:T(8,128)(2,1)S(1)}, u32[]{:S(2)}, u32[]{:S(2)}) collective-permute-start(bf16[328,768]{1,0:T(8,128)(2,1)S(1)} %fusion), channel_id=1, source_target_pairs={{0,8},{4,12},{8,0},{12,4},{16,24},{20,28},{24,16},{28,20},{1,9},{5... | collective-permute-start | bytes 1511432 | tf_op jit(solution)/shard_map/ppermute | solution.py:556
  247.3 19.9 %collective-permute-start.23 = (bf16[328,768]{1,0:T(8,128)(2,1)S(1)}, bf16[328,768]{1,0:T(8,128)(2,1)S(1)}, u32[]{:S(2)}, u32[]{:S(2)}) collective-permute-start(bf16[328,768]{1,0:T(8,128)(2,1)S(1)} %fusion.1), channel_id=1, source_target_pairs={{0,16},{4,20},{8,24},{12,28},{16,0},{20,4},{24,8},{28,12},{1,17},{... | collective-permute-start | bytes 1511432 | tf_op jit(solution)/shard_map/ppermute | solution.py:556
  267.4 15.4 %collective-permute-start.24 = (f32[308,768]{1,0:T(8,128)S(1)}, f32[308,768]{1,0:T(8,128)S(1)}, u32[]{:S(2)}, u32[]{:S(2)}) collective-permute-start(f32[308,768]{1,0:T(8,128)S(1)} %pad_maximum_fusion.7), channel_id=1, source_target_pairs={{0,4},{4,0},{8,12},{12,8},{16,20},{20,16},{24,28},{28,24},{1,5},{5... | collective-permute-start | bytes 2838536 | tf_op jit(solution)/shard_map/ppermute | solution.py:556
  283.0 1.8 copy-start
  (3 other events, 2.5 us)
Sparse Core Ops, SparseCore 0:
  21.8 63.6 all-gather.5
  174.0 51.2 reduce-scatter.1
  227.4 40.3 all-gather.3
